TPU v7x, 32 devices: a whole 2x2x4 slice. The times are simulated.
32 devices in a mesh: ctx: 16 (over z, x, core), head: 2 (over y).
Axes of the slice: x: 2, y: 2, z: 4, core: 2. Of those that a mesh axis runs over, the one named last changes fastest.
Arguments:
- queries: bfloat16 [4096, 2048], P(('ctx', 'head')), may hold values from -8.5 to 8.5
- keys: bfloat16 [4096, 1024], P(('ctx', 'head')), may hold values from -8.5 to 8.5
- values: bfloat16 [4096, 1024], P(('ctx', 'head')), may hold values from -5 to 5
- grad_attn: bfloat16 [4096, 2048], P(('ctx', 'head')), may hold values from -5 to 5
- parent_gap: int32 [16], replicated, may hold values from 0 to 2, as said below
Outputs:
- attended: bfloat16 [4096, 2048], P(('ctx', 'head'))
- grad_query: bfloat16 [4096, 2048], P(('ctx', 'head'))
- grad_key: bfloat16 [4096, 1024], P(('ctx', 'head'))
- grad_value: bfloat16 [4096, 1024], P(('ctx', 'head'))
Inputs may be any that keep to these rules, and one draw needn't show every extreme that they name: Shards are in depth-first order of a tree rooted at shard 0: the parent of shard s > 0 is shard s - parent_gap[s], and parent_gap[0] = 0. The ancestor 4 levels above a shard, where it exists, lies at most 8 shards before it.
All inputs are finite; a program needn't handle non-finite values.
Results may differ from a plain program's by a relative error of at most 0.011.
Values may be sent and summed in bfloat16 or wider, within the bound.
A program may use at most 128 MiB of HBM per device.

v0:
```python
import math

import jax
import jax.numpy as jnp
from jax import lax
from jax.sharding import PartitionSpec as P

HD = 256
GROUP = 2
WINDOW = 1024
FORK = 2


BASE = 10000.0


def from_behind(block, axis, distance):
    devices = range(lax.axis_size(axis))
    route = [(i - distance, i) for i in devices if i - distance in devices]
    return lax.ppermute(block, axis, route)


def tree_tables(parent_gap):
    shard_count = parent_gap.shape[0]
    ordinal = jnp.arange(shard_count, dtype=jnp.int32)
    parent = jnp.where(parent_gap > 0, ordinal - parent_gap, shard_count)
    pointer = jnp.concatenate([parent, jnp.full((1,), shard_count, jnp.int32)])
    depths = jnp.concatenate([(parent_gap > 0).astype(jnp.int32), jnp.zeros((1,), jnp.int32)])
    jumped = pointer
    for rounds in range(shard_count.bit_length()):
        depths = depths + jnp.take(depths, jumped)
        jumped = jnp.take(jumped, jumped)
    return (pointer, depths)


def rotate(inputs, position, direction):
    half_dim = inputs.shape[-1] // 2
    frequency = jnp.exp(
        jnp.arange(half_dim, dtype=jnp.float32) * (-2.0 * math.log(BASE) / inputs.shape[-1])
    )
    angles = position.astype(jnp.float32)[:, None] * frequency[None, :]
    cosine = jnp.cos(angles)[:, None, :]
    sine_part = direction * jnp.sin(angles)[:, None, :]
    first_half = inputs[..., :half_dim]
    second = inputs[..., half_dim:]
    return jnp.concatenate(
        [first_half * cosine - second * sine_part, second * cosine + first_half * sine_part], -1
    )


def visible_mask(length, levels, present):
    within = jnp.arange(length, dtype=jnp.int32)
    later_key = within[None, :] > within[:, None]
    blocks_list = [jnp.logical_not(later_key)]
    for height in range(1, levels + 1):
        blocks_list.append(
            jnp.logical_and(present[height - 1], jnp.logical_or(height < levels, later_key))
        )
    return jnp.stack(blocks_list, 1).reshape(length, (levels + 1) * length)


def attend(query, key_all, value_all, grad_out, visible):
    scaling = query.shape[-1] ** (-0.5)
    scores = (
        jnp.einsum("tkgd,ukd->kgtu", query, key_all, preferred_element_type=jnp.float32) * scaling
    )
    scores = jnp.where(visible, scores, -1e30)
    highest = jnp.max(scores, -1, keepdims=True)
    raw_weights = jnp.where(visible, jnp.exp(scores - highest), 0.0)
    probabilities = raw_weights / jnp.sum(raw_weights, -1, keepdims=True)
    probs_low = probabilities.astype(jnp.bfloat16)
    attended = jnp.einsum(
        "kgtu,ukd->tkgd", probs_low, value_all, preferred_element_type=jnp.float32
    ).astype(jnp.bfloat16)
    grad_prob = jnp.einsum(
        "tkgd,ukd->kgtu", grad_out, value_all, preferred_element_type=jnp.float32
    )
    row_delta = jnp.sum(probabilities * grad_prob, -1, keepdims=True)
    grad_score = (probabilities * (grad_prob - row_delta) * scaling).astype(jnp.bfloat16)
    grad_qrot = jnp.einsum(
        "kgtu,ukd->tkgd", grad_score, key_all, preferred_element_type=jnp.float32
    )
    part_key = jnp.einsum("kgtu,tkgd->ukd", grad_score, query, preferred_element_type=jnp.float32)
    part_value = jnp.einsum(
        "kgtu,tkgd->ukd", probs_low, grad_out, preferred_element_type=jnp.float32
    )
    return (attended, grad_qrot, part_key, part_value)


def shards(queries, keys, values, grad_attn, parent_gap):
    query_in, key_in, value_in, grad_in = (
        lax.all_to_all(queries, "head", split_axis=1, concat_axis=0, tiled=True),
        lax.all_to_all(keys, "head", split_axis=1, concat_axis=0, tiled=True),
        lax.all_to_all(values, "head", split_axis=1, concat_axis=0, tiled=True),
        lax.all_to_all(grad_attn, "head", split_axis=1, concat_axis=0, tiled=True),
    )
    tokens = query_in.shape[0]
    kv_local = key_in.shape[1] // HD
    levels = WINDOW // tokens
    reach = levels * FORK
    shard_count = lax.axis_size("ctx")
    own_shard = lax.axis_index("ctx")
    pointer, depths = tree_tables(parent_gap)
    within = jnp.arange(tokens, dtype=jnp.int32)
    position = jnp.take(depths, own_shard) * tokens + within
    query_rot = rotate(
        query_in.astype(jnp.float32).reshape(tokens, kv_local * GROUP, HD), position, 1.0
    ).astype(jnp.bfloat16)
    query_rot = query_rot.reshape(tokens, kv_local, GROUP, HD)
    key_rot = rotate(
        key_in.astype(jnp.float32).reshape(tokens, kv_local, HD), position, 1.0
    ).astype(jnp.bfloat16)
    value_own = value_in.reshape(tokens, kv_local, HD)
    grad_out = grad_in.reshape(tokens, kv_local, GROUP, HD)
    elders = []
    current = jnp.take(pointer, own_shard)
    for height in range(levels):
        elders.append(current)
        current = jnp.take(pointer, current)
    elders = jnp.stack(elders)
    present = elders < shard_count
    slot_index = jnp.where(present, own_shard - elders, 0)
    chosen = jnp.concatenate([jnp.zeros((1,), jnp.int32), slot_index])
    sections = []
    stride = 1
    while stride <= reach:
        amount = min(stride, reach + 1 - stride)
        sections.append((stride, amount))
        stride = stride + amount
    key_list = [key_rot]
    value_list = [value_own]
    for offset in range(1, reach + 1):
        got_key, got_value = from_behind((key_rot, value_own), "ctx", offset)
        key_list.append(got_key)
        value_list.append(got_value)
    stack_key = jnp.stack(key_list)
    stack_value = jnp.stack(value_list)
    key_all = jnp.take(stack_key, chosen, axis=0).reshape((levels + 1) * tokens, kv_local, HD)
    value_all = jnp.take(stack_value, chosen, axis=0).reshape((levels + 1) * tokens, kv_local, HD)
    visible = visible_mask(tokens, levels, present)
    attended, grad_qrot, part_key, part_value = attend(
        query_rot, key_all, value_all, grad_out, visible
    )
    attended_out = lax.all_to_all(
        attended.reshape(tokens, kv_local * GROUP * HD),
        "head",
        split_axis=0,
        concat_axis=1,
        tiled=True,
    )
    empty = jnp.zeros((reach + 1, tokens, kv_local, HD), jnp.float32)
    return_key = empty.at[chosen].add(part_key.reshape(levels + 1, tokens, kv_local, HD))
    return_value = empty.at[chosen].add(part_value.reshape(levels + 1, tokens, kv_local, HD))
    for stride, amount in reversed(sections):
        got_key, got_value = from_behind(
            (return_key[stride : stride + amount], return_value[stride : stride + amount]),
            "ctx",
            -stride,
        )
        return_key = return_key.at[:amount].add(got_key)
        return_value = return_value.at[:amount].add(got_value)
    total_key = return_key[0]
    total_value = return_value[0]
    grad_query = rotate(grad_qrot.reshape(tokens, kv_local * GROUP, HD), position, -1.0).astype(
        jnp.bfloat16
    )
    grad_key = rotate(total_key, position, -1.0).astype(jnp.bfloat16)
    grad_value = total_value.astype(jnp.bfloat16)
    query_back, key_back, value_back = (
        lax.all_to_all(
            grad_query.reshape(tokens, kv_local * GROUP * HD),
            "head",
            split_axis=0,
            concat_axis=1,
            tiled=True,
        ),
        lax.all_to_all(
            grad_key.reshape(tokens, kv_local * HD), "head", split_axis=0, concat_axis=1, tiled=True
        ),
        lax.all_to_all(
            grad_value.reshape(tokens, kv_local * HD),
            "head",
            split_axis=0,
            concat_axis=1,
            tiled=True,
        ),
    )
    return (attended_out, query_back, key_back, value_back)


def solution(mesh):
    in_specs = (
        P(("ctx", "head"), None),
        P(("ctx", "head"), None),
        P(("ctx", "head"), None),
        P(("ctx", "head"), None),
        P(),
    )
    out_specs = (
        P(("ctx", "head"), None),
        P(("ctx", "head"), None),
        P(("ctx", "head"), None),
        P(("ctx", "head"), None),
    )
    return jax.shard_map(shards, mesh=mesh, in_specs=in_specs, out_specs=out_specs, check_vma=False)
```

profile of v0, /device:TPU:24, one launch (start us, length us, event | category | flops | bytes accessed | tf_op | source)
XLA Modules:
  0.0 407.2 jit_solution(17301536102874395599)
XLA Ops:
  0.6 1.7 copy.174
  2.3 3.4 all-to-all-start.1
  27.2 3.5 all-to-all-start
  32.0 1.9 collective-permute-start.8
  33.9 3.4 collective-permute-start.9
  37.4 1.9 collective-permute-start.10
  41.9 3.5 all-to-all-start.2
  47.7 5.8 %all-to-all-done.2 = bf16[128,2,1024]{2,0,1:T(8,128)(2,1)S(1)} async-done(((bf16[128,2,1024]{2,0,1:T(8,128)(2,1)}), bf16[128,2,1024]{2,0,1:T(8,128)(2,1)S(1)}, u32[]{:S(2)}, u32[]{:S(2)}) %all-to-all-start.2) | async-done | bytes 524320 | tf_op jit(solution)/shard_map/all_to_all | solution.py:92
  53.6 3.5 all-to-all-start.4
  59.5 4.9 %all-to-all-done.4 = bf16[128,2,1024]{2,0,1:T(8,128)(2,1)S(1)} async-done(((bf16[128,2,1024]{2,0,1:T(8,128)(2,1)}), bf16[128,2,1024]{2,0,1:T(8,128)(2,1)S(1)}, u32[]{:S(2)}, u32[]{:S(2)}) %all-to-all-start.4) | async-done | bytes 524320 | tf_op jit(solution)/shard_map/all_to_all | solution.py:95
  66.0 1.7 bitcast_dynamic-update-slice_fusion.7
  69.0 1.7 bitcast_dynamic-update-slice_fusion.6
  71.9 1.7 bitcast_dynamic-update-slice_fusion.5
  73.6 1.9 collective-permute-start
  75.5 1.7 bitcast_dynamic-update-slice_fusion.4
  77.2 1.9 collective-permute-start.1
  79.1 1.7 bitcast_dynamic-update-slice_fusion.3
  80.8 15.9 %collective-permute-done.13 = bf16[256,2,256]{2,0,1:T(8,128)(2,1)S(1)} collective-permute-done((bf16[256,2,256]{2,0,1:T(8,128)(2,1)}, bf16[256,2,256]{2,0,1:T(8,128)(2,1)S(1)}, u32[]{:S(2)}, u32[]{:S(2)}) %collective-permute-start.13) | collective-permute-done | bytes 262176 | tf_op jit(solution)/shard_map/ppermute | solution.py:20
  96.7 1.9 collective-permute-start.2
  107.4 1.5 collective-permute-start.7
  110.3 41.3 %collective-permute-done.4 = bf16[256,2,256]{2,0,1:T(8,128)(2,1)S(1)} collective-permute-done((bf16[256,2,256]{2,0,1:T(8,128)(2,1)S(1)}, bf16[256,2,256]{2,0,1:T(8,128)(2,1)S(1)}, u32[]{:S(2)}, u32[]{:S(2)}) %collective-permute-start.4) | collective-permute-done | bytes 262176 | tf_op jit(solution)/shard_map/ppermute | solution.py:20
  152.4 3.3 collective-permute-done.5
  156.3 2.3 gather_fusion.10
  160.1 2.3 gather_fusion
  163.0 3.3 fusion.25
  166.3 4.6 %fusion.7 = (f32[2,2,256]{2,1,0:T(2,128)S(1)}, f32[2,2,256,1280]{2,3,1,0:T(8,128)}) fusion(pred[256,1280]{0,1:T(8,128)(4,1)S(1)} %bitcast.201, bf16[1280,2,256,1]{2,0,3,1:T(8,128)(2,1)S(1)} %bitcast.174, bf16[256,2,2,128]{3,0,2,1:T(8,128)(2,1)S(1)} %bitcast.190, bf16[256,2,2,128]{3,0,2,1:T(8,128)(2,1)S(1)} %bitcast.196), kind=kOutput, calls=%fused_computation.24 | convolution fusion | flops 678692096 | bytes 7409664 | tf_op jit(solution)/shard_map/sub | solution.py:69
  170.9 11.0 %convolution_bitcast_fusion = f32[1280,2,256]{0,2,1:T(8,128)S(1)} fusion(f32[2,1280,256,2]{2,1,3,0:T(8,128)} %fusion.25, bf16[256,2,2,128]{3,0,2,1:T(8,128)(2,1)S(1)} %bitcast.191, bf16[256,2,2,128]{3,0,2,1:T(8,128)(2,1)} %bitcast.193, f32[2,2,256,1280]{2,3,1,0:T(8,128)} %get-tuple-element.204, f32[2,2,256]{2,1,0:T(2,128)S(1)} %get-tuple-element.203, ...), kind=kOutput, calls=%fused_computation.25 | convolution fusion | flops 683936000 | bytes 13963264 | tf_op jit(solution)/shard_map/kgtu,tkgd->ukd/dot_general | solution.py:83
  181.9 2.2 copy.125
  184.1 2.0 copy.126
  186.1 2.7 broadcast_in_dim.81.clone
  188.8 7.5 %scatter_fusion = f32[9,256,2,256]{3,1,2,0:T(8,128)} fusion(f32[9,256,2,256]{3,1,2,0:T(8,128)} %broadcast_in_dim.81.clone, s32[5]{0:T(128)S(1)} %fusion.33, f32[5,256,2,256]{3,1,2,0:T(8,128)S(1)} %copy.126), kind=kCustom, calls=%fused_computation.11 | custom fusion | flops 655360 | bytes 7864340 | tf_op jit(solution)/shard_map/scatter-add | solution.py:152
  196.3 1.9 slice.384
  198.2 2.1 collective-permute-start.16
  200.3 5.9 %fusion.10 = f32[2,1280,256,1]{2,1,3,0:T(8,128)} fusion(bf16[256,2,2,256]{3,2,1,0:T(2,128)(2,1)S(1)} %reshape.666, f32[2,2,256]{2,1,0:T(2,128)S(1)} %get-tuple-element.203, pred[256,1280]{0,1:T(8,128)(4,1)} %bitcast.198, bf16[1280,2,256,1]{2,0,3,1:T(8,128)(2,1)} %bitcast.175, bf16[256,2,2,128]{3,0,2,1:T(8,128)(2,1)S(1)} %bitcast.192, ...), kind=kOutput, calls=%fused_computation.30 | convolution fusion | flops 1351092480 | bytes 5312512 | tf_op jit(solution)/shard_map/kgtu,tkgd->ukd/dot_general | solution.py:84
  206.1 2.0 copy.130
  208.2 2.6 broadcast_in_dim.81.clone.1
  210.8 7.5 %scatter_fusion.1 = f32[9,256,2,256]{3,1,2,0:T(8,128)} fusion(f32[9,256,2,256]{3,1,2,0:T(8,128)} %broadcast_in_dim.81.clone.1, s32[5]{0:T(128)S(1)} %fusion.33, f32[5,256,2,256]{3,1,2,0:T(8,128)S(1)} %copy.130), kind=kCustom, calls=%fused_computation.12 | custom fusion | flops 655360 | bytes 7864340 | tf_op jit(solution)/shard_map/scatter-add | solution.py:153
  220.7 2.0 fusion.23
  222.8 1.7 slice.386
  224.5 1.4 collective-permute-start.17
  225.9 5.3 %collective-permute-done.20 = f32[1,256,2,256]{3,1,2,0:T(8,128)S(1)} collective-permute-done((f32[1,256,2,256]{3,1,2,0:T(8,128)S(1)}, f32[1,256,2,256]{3,1,2,0:T(8,128)S(1)}, u32[]{:S(2)}, u32[]{:S(2)}) %collective-permute-start.20) | collective-permute-done | bytes 524320 | tf_op jit(solution)/shard_map/ppermute | solution.py:20
  231.2 1.9 fusion.21
  233.1 1.8 slice.396
  235.0 2.8 collective-permute-start.21
  237.8 38.4 %collective-permute-done.17 = f32[4,256,2,256]{3,1,2,0:T(8,128)S(1)} collective-permute-done((f32[4,256,2,256]{3,1,2,0:T(8,128)S(1)}, f32[4,256,2,256]{3,1,2,0:T(8,128)S(1)}, u32[]{:S(2)}, u32[]{:S(2)}) %collective-permute-start.17) | collective-permute-done | bytes 2097184 | tf_op jit(solution)/shard_map/ppermute | solution.py:20
  276.2 2.0 slice_add_fusion.1
  280.7 14.1 %collective-permute-start.18 = (f32[2,256,2,256]{3,1,2,0:T(8,128)}, f32[2,256,2,256]{3,1,2,0:T(8,128)}, u32[]{:S(2)}, u32[]{:S(2)}) collective-permute-start(f32[2,256,2,256]{3,1,2,0:T(8,128)} %slice.388), channel_id=1, source_target_pairs={{4,0},{6,2},{8,4},{10,6},{12,8},{14,10},{16,12},{18,14},{20,16},{2... | collective-permute-start | bytes 3145736 | tf_op jit(solution)/shard_map/ppermute | solution.py:20
  294.9 11.7 %fusion.9 = f32[2,256,2,256]{3,1,2,0:T(8,128)} fusion(bf16[1280,2,256,1]{2,0,3,1:T(8,128)(2,1)S(1)} %bitcast.177, f32[2,1280,256,2]{2,1,3,0:T(8,128)} %fusion.25, f32[2,2,256,1280]{2,3,1,0:T(8,128)} %get-tuple-element.204, f32[2,2,256]{2,1,0:T(2,128)S(1)} %get-tuple-element.203, pred[256,1280]{0,1:T(8,128)(4,1)} %bitcast.199), kind=kOutput, calls=%fused_computation.27 | convolution fusion | flops 682887424 | bytes 13176832 | tf_op jit(solution)/shard_map/kgtu,ukd->tkgd/dot_general | solution.py:80
  306.6 14.5 %collective-permute-done.21 = f32[4,256,2,256]{3,1,2,0:T(8,128)} collective-permute-done((f32[4,256,2,256]{3,1,2,0:T(8,128)S(1)}, f32[4,256,2,256]{3,1,2,0:T(8,128)}, u32[]{:S(2)}, u32[]{:S(2)}) %collective-permute-start.21) | collective-permute-done | bytes 2097184 | tf_op jit(solution)/shard_map/ppermute | solution.py:20
  321.1 2.6 slice_add_fusion
  324.7 14.4 %collective-permute-start.22 = (f32[2,256,2,256]{3,1,2,0:T(8,128)}, f32[2,256,2,256]{3,1,2,0:T(8,128)}, u32[]{:S(2)}, u32[]{:S(2)}) collective-permute-start(f32[2,256,2,256]{3,1,2,0:T(8,128)} %slice.398), channel_id=1, source_target_pairs={{4,0},{6,2},{8,4},{10,6},{12,8},{14,10},{16,12},{18,14},{20,16},{2... | collective-permute-start | bytes 3145736 | tf_op jit(solution)/shard_map/ppermute | solution.py:20
  339.1 5.5 %fusion.17 = bf16[256,2,2,256]{0,3,2,1:T(8,128)(2,1)} fusion(bf16[1280,2,256,1]{2,0,3,1:T(8,128)(2,1)S(1)} %bitcast.167, f32[2,2,256]{2,1,0:T(2,128)S(1)} %get-tuple-element.203, pred[256,1280]{0,1:T(8,128)(4,1)} %bitcast.200, bf16[1280,2,256,1]{2,0,3,1:T(8,128)(2,1)} %bitcast.176, bf16[256,2,2,128]{3,0,2,1:T(8,128)(2,1)} %bitcast.189, ...), kind=kOutput, calls=%fused_computation.37 | convolution fusion | flops 1351354624 | bytes 4001792 | tf_op jit(solution)/shard_map/kgtu,ukd->tkgd/dot_general | solution.py:72
  346.6 4.2 %all-to-all-start.3 = ((bf16[2,128,1024]{1,2,0:T(8,128)(2,1)}), bf16[2,128,1024]{1,2,0:T(8,128)(2,1)}, u32[]{:S(2)}, u32[]{:S(2)}) async-start(bf16[2,128,1024]{1,2,0:T(8,128)(2,1)} %copy.115), calls=%async_computation.3 | async-start | bytes 1048576 | tf_op jit(solution)/shard_map/all_to_all | solution.py:144
  354.2 1.8 slice_add_fusion.3
  356.8 1.9 collective-permute-start.19
  360.1 2.2 convert_element_type.84
  362.3 3.8 collective-permute-done.22
  369.3 8.5 %collective-permute-start.23 = (f32[1,256,2,256]{3,1,2,0:T(8,128)}, f32[1,256,2,256]{3,1,2,0:T(8,128)}, u32[]{:S(2)}, u32[]{:S(2)}) collective-permute-start(f32[1,256,2,256]{3,1,2,0:T(8,128)} %slice.400), channel_id=1, source_target_pairs={{2,0},{4,2},{6,4},{8,6},{10,8},{12,10},{14,12},{16,14},{18,16},{20... | collective-permute-start | bytes 1572872 | tf_op jit(solution)/shard_map/ppermute | solution.py:20
  378.9 3.5 all-to-all-start.5
  383.7 5.3 %all-to-all-done.5 = bf16[2,128,1024]{2,1,0:T(8,128)(2,1)S(1)} async-done(((bf16[2,128,1024]{2,1,0:T(8,128)(2,1)}), bf16[2,128,1024]{2,1,0:T(8,128)(2,1)S(1)}, u32[]{:S(2)}, u32[]{:S(2)}) %all-to-all-start.5) | async-done | bytes 524320 | tf_op jit(solution)/shard_map/all_to_all | solution.py:170
  389.0 3.4 all-to-all-start.6
  394.7 2.9 all-to-all-done.6
  397.6 3.4 all-to-all-start.7
  401.0 2.0 copy.133
  (170 shorter events, 70.1 us)
Async XLA Ops:
  2.3 24.8 %all-to-all-start.1 = ((bf16[128,2,512]{2,0,1:T(8,128)(2,1)}), bf16[128,2,512]{2,0,1:T(8,128)(2,1)S(1)}, u32[]{:S(2)}, u32[]{:S(2)}) async-start(bf16[128,2,512]{2,0,1:T(8,128)(2,1)} %bitcast.163), calls=%async_computation.1 | async-start | bytes 524288 | tf_op jit(solution)/shard_map/all_to_all | solution.py:93
  12.2 11.8 %copy-start.12 = (bf16[128,1024]{1,0:T(8,128)(2,1)S(1)}, bf16[128,1024]{1,0:T(8,128)(2,1)}, u32[]{:S(2)}) copy-start(bf16[128,1024]{1,0:T(8,128)(2,1)} %param.27) | copy-start | bytes 786436
  13.0 11.8 %copy-start.10 = (bf16[128,2048]{1,0:T(8,128)(2,1)S(1)}, bf16[128,2048]{1,0:T(8,128)(2,1)}, u32[]{:S(2)}) copy-start(bf16[128,2048]{1,0:T(8,128)(2,1)} %param.25) | copy-start | bytes 1572868
  14.5 11.1 %copy-start.11 = (bf16[128,2048]{1,0:T(8,128)(2,1)S(1)}, bf16[128,2048]{1,0:T(8,128)(2,1)}, u32[]{:S(2)}) copy-start(bf16[128,2048]{1,0:T(8,128)(2,1)} %param.28) | copy-start | bytes 1572868
  27.1 14.8 %copy-start.16 = (pred[256,5,256]{0,2,1:T(8,128)(4,1)}, pred[256,5,256]{0,2,1:T(8,128)(4,1)S(1)}, u32[]{:S(2)}) copy-start(pred[256,5,256]{0,2,1:T(8,128)(4,1)S(1)} %fusion.30) | copy-start | bytes 983044
  27.2 14.7 %all-to-all-start = ((bf16[128,2,512]{2,0,1:T(8,128)(2,1)}), bf16[128,2,512]{2,0,1:T(8,128)(2,1)S(1)}, u32[]{:S(2)}, u32[]{:S(2)}) async-start(bf16[128,2,512]{2,0,1:T(8,128)(2,1)} %bitcast.164), calls=%async_computation | async-start | bytes 524288 | tf_op jit(solution)/shard_map/all_to_all | solution.py:94
  32.0 32.7 %collective-permute-start.8 = (bf16[256,2,256]{2,0,1:T(8,128)(2,1)}, bf16[256,2,256]{2,0,1:T(8,128)(2,1)}, u32[]{:S(2)}, u32[]{:S(2)}) collective-permute-start(bf16[256,2,256]{2,0,1:T(8,128)(2,1)} %pad_maximum_fusion.2), channel_id=1, source_target_pairs={{0,2},{2,4},{4,6},{6,8},{8,10},{10,12},{12,14},{14,16},{16,18},{18... | collective-permute-start | bytes 786440 | tf_op jit(solution)/shard_map/ppermute | solution.py:20
  33.9 33.8 %collective-permute-start.9 = (bf16[256,2,256]{2,0,1:T(8,128)(2,1)}, bf16[256,2,256]{2,0,1:T(8,128)(2,1)}, u32[]{:S(2)}, u32[]{:S(2)}) collective-permute-start(bf16[256,2,256]{2,0,1:T(8,128)(2,1)} %pad_maximum_fusion.2), channel_id=1, source_target_pairs={{0,4},{2,6},{4,8},{6,10},{8,12},{10,14},{12,16},{14,18},{16,20},{1... | collective-permute-start | bytes 786440 | tf_op jit(solution)/shard_map/ppermute | solution.py:20
  37.4 33.3 %collective-permute-start.10 = (bf16[256,2,256]{2,0,1:T(8,128)(2,1)}, bf16[256,2,256]{2,0,1:T(8,128)(2,1)}, u32[]{:S(2)}, u32[]{:S(2)}) collective-permute-start(bf16[256,2,256]{2,0,1:T(8,128)(2,1)} %pad_maximum_fusion.2), channel_id=1, source_target_pairs={{0,6},{2,8},{4,10},{6,12},{8,14},{10,16},{12,18},{14,20},{16,22},{... | collective-permute-start | bytes 786440 | tf_op jit(solution)/shard_map/ppermute | solution.py:20
  39.3 34.3 %collective-permute-start.11 = (bf16[256,2,256]{2,0,1:T(8,128)(2,1)}, bf16[256,2,256]{2,0,1:T(8,128)(2,1)}, u32[]{:S(2)}, u32[]{:S(2)}) collective-permute-start(bf16[256,2,256]{2,0,1:T(8,128)(2,1)} %pad_maximum_fusion.2), channel_id=1, source_target_pairs={{0,8},{2,10},{4,12},{6,14},{8,16},{10,18},{12,20},{14,22},{16,24},... | collective-permute-start | bytes 786440 | tf_op jit(solution)/shard_map/ppermute | solution.py:20
  40.6 36.6 %collective-permute-start.12 = (bf16[256,2,256]{2,0,1:T(8,128)(2,1)}, bf16[256,2,256]{2,0,1:T(8,128)(2,1)}, u32[]{:S(2)}, u32[]{:S(2)}) collective-permute-start(bf16[256,2,256]{2,0,1:T(8,128)(2,1)} %pad_maximum_fusion.2), channel_id=1, source_target_pairs={{0,10},{2,12},{4,14},{6,16},{8,18},{10,20},{12,22},{14,24},{16,26}... | collective-permute-start | bytes 786440 | tf_op jit(solution)/shard_map/ppermute | solution.py:20
  41.9 11.7 %all-to-all-start.2 = ((bf16[128,2,1024]{2,0,1:T(8,128)(2,1)}), bf16[128,2,1024]{2,0,1:T(8,128)(2,1)S(1)}, u32[]{:S(2)}, u32[]{:S(2)}) async-start(bf16[128,2,1024]{2,0,1:T(8,128)(2,1)} %bitcast.162), calls=%async_computation.2 | async-start | bytes 1048576 | tf_op jit(solution)/shard_map/all_to_all | solution.py:92
  53.6 10.8 %all-to-all-start.4 = ((bf16[128,2,1024]{2,0,1:T(8,128)(2,1)}), bf16[128,2,1024]{2,0,1:T(8,128)(2,1)S(1)}, u32[]{:S(2)}, u32[]{:S(2)}) async-start(bf16[128,2,1024]{2,0,1:T(8,128)(2,1)} %bitcast.161), calls=%async_computation.4 | async-start | bytes 1048576 | tf_op jit(solution)/shard_map/all_to_all | solution.py:95
  57.7 15.9 %copy-start.15 = (bf16[256,2,256]{2,0,1:T(8,128)(2,1)S(1)}, bf16[256,2,256]{2,0,1:T(8,128)(2,1)}, u32[]{:S(2)}) copy-start(bf16[256,2,256]{2,0,1:T(8,128)(2,1)} %copy.96) | copy-start | bytes 786436
  64.7 32.0 %collective-permute-start.13 = (bf16[256,2,256]{2,0,1:T(8,128)(2,1)}, bf16[256,2,256]{2,0,1:T(8,128)(2,1)S(1)}, u32[]{:S(2)}, u32[]{:S(2)}) collective-permute-start(bf16[256,2,256]{2,0,1:T(8,128)(2,1)} %pad_maximum_fusion.2), channel_id=1, source_target_pairs={{0,12},{2,14},{4,16},{6,18},{8,20},{10,22},{12,24},{14,26},{16,28}... | collective-permute-start | bytes 786440 | tf_op jit(solution)/shard_map/ppermute | solution.py:20
  67.7 31.6 %collective-permute-start.14 = (bf16[256,2,256]{2,0,1:T(8,128)(2,1)}, bf16[256,2,256]{2,0,1:T(8,128)(2,1)S(1)}, u32[]{:S(2)}, u32[]{:S(2)}) collective-permute-start(bf16[256,2,256]{2,0,1:T(8,128)(2,1)} %pad_maximum_fusion.2), channel_id=1, source_target_pairs={{0,14},{2,16},{4,18},{6,20},{8,22},{10,24},{12,26},{14,28},{16,30}... | collective-permute-start | bytes 786440 | tf_op jit(solution)/shard_map/ppermute | solution.py:20
  70.7 30.7 %collective-permute-start.15 = (bf16[256,2,256]{2,0,1:T(8,128)(2,1)}, bf16[256,2,256]{2,0,1:T(8,128)(2,1)S(1)}, u32[]{:S(2)}, u32[]{:S(2)}) collective-permute-start(bf16[256,2,256]{2,0,1:T(8,128)(2,1)} %pad_maximum_fusion.2), channel_id=1, source_target_pairs={{0,16},{2,18},{4,20},{6,22},{8,24},{10,26},{12,28},{14,30},{1,17},... | collective-permute-start | bytes 786440 | tf_op jit(solution)/shard_map/ppermute | solution.py:20
  73.6 29.7 %collective-permute-start = (bf16[256,2,256]{2,0,1:T(8,128)(2,1)S(1)}, bf16[256,2,256]{2,0,1:T(8,128)(2,1)S(1)}, u32[]{:S(2)}, u32[]{:S(2)}) collective-permute-start(bf16[256,2,256]{2,0,1:T(8,128)(2,1)S(1)} %copy-done.15), channel_id=1, source_target_pairs={{0,2},{2,4},{4,6},{6,8},{8,10},{10,12},{12,14},{14,16},{16,18},{18... | collective-permute-start | bytes 786440 | tf_op jit(solution)/shard_map/ppermute | solution.py:20
  77.2 28.2 %collective-permute-start.1 = (bf16[256,2,256]{2,0,1:T(8,128)(2,1)S(1)}, bf16[256,2,256]{2,0,1:T(8,128)(2,1)S(1)}, u32[]{:S(2)}, u32[]{:S(2)}) collective-permute-start(bf16[256,2,256]{2,0,1:T(8,128)(2,1)S(1)} %copy-done.15), channel_id=1, source_target_pairs={{0,4},{2,6},{4,8},{6,10},{8,12},{10,14},{12,16},{14,18},{16,20},{1... | collective-permute-start | bytes 786440 | tf_op jit(solution)/shard_map/ppermute | solution.py:20
  96.7 10.7 %collective-permute-start.2 = (bf16[256,2,256]{2,0,1:T(8,128)(2,1)S(1)}, bf16[256,2,256]{2,0,1:T(8,128)(2,1)S(1)}, u32[]{:S(2)}, u32[]{:S(2)}) collective-permute-start(bf16[256,2,256]{2,0,1:T(8,128)(2,1)S(1)} %copy-done.15), channel_id=1, source_target_pairs={{0,6},{2,8},{4,10},{6,12},{8,14},{10,16},{12,18},{14,20},{16,22},{... | collective-permute-start | bytes 786440 | tf_op jit(solution)/shard_map/ppermute | solution.py:20
  99.3 10.3 %collective-permute-start.3 = (bf16[256,2,256]{2,0,1:T(8,128)(2,1)S(1)}, bf16[256,2,256]{2,0,1:T(8,128)(2,1)S(1)}, u32[]{:S(2)}, u32[]{:S(2)}) collective-permute-start(bf16[256,2,256]{2,0,1:T(8,128)(2,1)S(1)} %copy-done.15), channel_id=1, source_target_pairs={{0,8},{2,10},{4,12},{6,14},{8,16},{10,18},{12,20},{14,22},{16,24},... | collective-permute-start | bytes 786440 | tf_op jit(solution)/shard_map/ppermute | solution.py:20
  101.4 50.3 %collective-permute-start.4 = (bf16[256,2,256]{2,0,1:T(8,128)(2,1)S(1)}, bf16[256,2,256]{2,0,1:T(8,128)(2,1)S(1)}, u32[]{:S(2)}, u32[]{:S(2)}) collective-permute-start(bf16[256,2,256]{2,0,1:T(8,128)(2,1)S(1)} %copy-done.15), channel_id=1, source_target_pairs={{0,10},{2,12},{4,14},{6,16},{8,18},{10,20},{12,22},{14,24},{16,26}... | collective-permute-start | bytes 786440 | tf_op jit(solution)/shard_map/ppermute | solution.py:20
  103.4 52.3 %collective-permute-start.5 = (bf16[256,2,256]{2,0,1:T(8,128)(2,1)S(1)}, bf16[256,2,256]{2,0,1:T(8,128)(2,1)S(1)}, u32[]{:S(2)}, u32[]{:S(2)}) collective-permute-start(bf16[256,2,256]{2,0,1:T(8,128)(2,1)S(1)} %copy-done.15), channel_id=1, source_target_pairs={{0,12},{2,14},{4,16},{6,18},{8,20},{10,22},{12,24},{14,26},{16,28}... | collective-permute-start | bytes 786440 | tf_op jit(solution)/shard_map/ppermute | solution.py:20
  105.4 53.3 %collective-permute-start.6 = (bf16[256,2,256]{2,0,1:T(8,128)(2,1)S(1)}, bf16[256,2,256]{2,0,1:T(8,128)(2,1)S(1)}, u32[]{:S(2)}, u32[]{:S(2)}) collective-permute-start(bf16[256,2,256]{2,0,1:T(8,128)(2,1)S(1)} %copy-done.15), channel_id=1, source_target_pairs={{0,14},{2,16},{4,18},{6,20},{8,22},{10,24},{12,26},{14,28},{16,30}... | collective-permute-start | bytes 786440 | tf_op jit(solution)/shard_map/ppermute | solution.py:20
  107.4 52.0 %collective-permute-start.7 = (bf16[256,2,256]{2,0,1:T(8,128)(2,1)S(1)}, bf16[256,2,256]{2,0,1:T(8,128)(2,1)S(1)}, u32[]{:S(2)}, u32[]{:S(2)}) collective-permute-start(bf16[256,2,256]{2,0,1:T(8,128)(2,1)S(1)} %copy-done.15), channel_id=1, source_target_pairs={{0,16},{2,18},{4,20},{6,22},{8,24},{10,26},{12,28},{14,30},{1,17},... | collective-permute-start | bytes 786440 | tf_op jit(solution)/shard_map/ppermute | solution.py:20
  162.8 3.4 copy-start.1
  162.9 3.3 copy-start.7
  162.9 3.3 copy-start.13
  163.0 3.3 copy-start.14
  163.0 3.3 copy-start.17
  198.2 22.5 %collective-permute-start.16 = (f32[1,256,2,256]{3,1,2,0:T(8,128)}, f32[1,256,2,256]{3,1,2,0:T(8,128)}, u32[]{:S(2)}, u32[]{:S(2)}) collective-permute-start(f32[1,256,2,256]{3,1,2,0:T(8,128)} %slice.384), channel_id=1, source_target_pairs={{16,0},{18,2},{20,4},{22,6},{24,8},{26,10},{28,12},{30,14},{17,1},... | collective-permute-start | bytes 1572872 | tf_op jit(solution)/shard_map/ppermute | solution.py:20
  219.4 11.8 %collective-permute-start.20 = (f32[1,256,2,256]{3,1,2,0:T(8,128)S(1)}, f32[1,256,2,256]{3,1,2,0:T(8,128)S(1)}, u32[]{:S(2)}, u32[]{:S(2)}) collective-permute-start(f32[1,256,2,256]{3,1,2,0:T(8,128)S(1)} %slice.394), channel_id=1, source_target_pairs={{16,0},{18,2},{20,4},{22,6},{24,8},{26,10},{28,12},{30,14},{17,1},... | collective-permute-start | bytes 1572872 | tf_op jit(solution)/shard_map/ppermute | solution.py:20
  224.5 51.6 %collective-permute-start.17 = (f32[4,256,2,256]{3,1,2,0:T(8,128)S(1)}, f32[4,256,2,256]{3,1,2,0:T(8,128)S(1)}, u32[]{:S(2)}, u32[]{:S(2)}) collective-permute-start(f32[4,256,2,256]{3,1,2,0:T(8,128)S(1)} %slice.386), channel_id=1, source_target_pairs={{8,0},{10,2},{12,4},{14,6},{16,8},{18,10},{20,12},{22,14},{24,16},... | collective-permute-start | bytes 6291464 | tf_op jit(solution)/shard_map/ppermute | solution.py:20
  235.0 59.9 %copy-start.8 = (bf16[5,256,2,256]{3,1,0,2:T(8,128)(2,1)S(1)}, bf16[5,256,2,256]{3,1,0,2:T(8,128)(2,1)}, u32[]{:S(2)}) copy-start(bf16[5,256,2,256]{3,1,0,2:T(8,128)(2,1)} %copy-done.7) | copy-start | bytes 3932164
  235.0 86.1 %collective-permute-start.21 = (f32[4,256,2,256]{3,1,2,0:T(8,128)S(1)}, f32[4,256,2,256]{3,1,2,0:T(8,128)}, u32[]{:S(2)}, u32[]{:S(2)}) collective-permute-start(f32[4,256,2,256]{3,1,2,0:T(8,128)S(1)} %slice.396), channel_id=1, source_target_pairs={{8,0},{10,2},{12,4},{14,6},{16,8},{18,10},{20,12},{22,14},{24,16},... | collective-permute-start | bytes 6291464 | tf_op jit(solution)/shard_map/ppermute | solution.py:20
  278.1 1.4 copy-start
  280.7 73.5 %collective-permute-start.18 = (f32[2,256,2,256]{3,1,2,0:T(8,128)}, f32[2,256,2,256]{3,1,2,0:T(8,128)}, u32[]{:S(2)}, u32[]{:S(2)}) collective-permute-start(f32[2,256,2,256]{3,1,2,0:T(8,128)} %slice.388), channel_id=1, source_target_pairs={{4,0},{6,2},{8,4},{10,6},{12,8},{14,10},{16,12},{18,14},{20,16},{2... | collective-permute-start | bytes 3145736 | tf_op jit(solution)/shard_map/ppermute | solution.py:20
  306.6 32.5 %copy-start.2 = (bf16[5,256,2,256]{3,1,0,2:T(8,128)(2,1)S(1)}, bf16[5,256,2,256]{3,1,0,2:T(8,128)(2,1)}, u32[]{:S(2)}) copy-start(bf16[5,256,2,256]{3,1,0,2:T(8,128)(2,1)} %copy-done.1) | copy-start | bytes 3932164
  324.7 41.4 %collective-permute-start.22 = (f32[2,256,2,256]{3,1,2,0:T(8,128)}, f32[2,256,2,256]{3,1,2,0:T(8,128)}, u32[]{:S(2)}, u32[]{:S(2)}) collective-permute-start(f32[2,256,2,256]{3,1,2,0:T(8,128)} %slice.398), channel_id=1, source_target_pairs={{4,0},{6,2},{8,4},{10,6},{12,8},{14,10},{16,12},{18,14},{20,16},{2... | collective-permute-start | bytes 3145736 | tf_op jit(solution)/shard_map/ppermute | solution.py:20
  346.6 32.3 %all-to-all-start.3 = ((bf16[2,128,1024]{1,2,0:T(8,128)(2,1)}), bf16[2,128,1024]{1,2,0:T(8,128)(2,1)}, u32[]{:S(2)}, u32[]{:S(2)}) async-start(bf16[2,128,1024]{1,2,0:T(8,128)(2,1)} %copy.115), calls=%async_computation.3 | async-start | bytes 1048576 | tf_op jit(solution)/shard_map/all_to_all | solution.py:144
  353.2 5.6 %copy-start.9 = (f32[256,128]{1,0:T(8,128)S(1)}, f32[256,128]{1,0:T(8,128)}, u32[]{:S(2)}) copy-start(f32[256,128]{1,0:T(8,128)} %get-tuple-element.187) | copy-start | bytes 393220
  354.2 4.6 %copy-start.5 = (f32[256,4,128]{2,1,0:T(4,128)S(1)}, f32[256,4,128]{2,1,0:T(4,128)}, u32[]{:S(2)}) copy-start(f32[256,4,128]{2,1,0:T(4,128)} %copy.154) | copy-start | bytes 1572868
  354.2 4.6 %copy-start.6 = (f32[256,4,128]{2,1,0:T(4,128)S(1)}, f32[256,4,128]{2,1,0:T(4,128)}, u32[]{:S(2)}) copy-start(f32[256,4,128]{2,1,0:T(4,128)} %copy.153) | copy-start | bytes 1572868
  356.8 21.0 %collective-permute-start.19 = (f32[1,256,2,256]{3,1,2,0:T(8,128)}, f32[1,256,2,256]{3,1,2,0:T(8,128)}, u32[]{:S(2)}, u32[]{:S(2)}) collective-permute-start(f32[1,256,2,256]{3,1,2,0:T(8,128)} %slice.390), channel_id=1, source_target_pairs={{2,0},{4,2},{6,4},{8,6},{10,8},{12,10},{14,12},{16,14},{18,16},{20... | collective-permute-start | bytes 1572872 | tf_op jit(solution)/shard_map/ppermute | solution.py:20
  367.5 1.0 copy-start.3
  369.3 23.1 %copy-start.4 = (f32[2,256,2,256]{3,1,2,0:T(8,128)S(1)}, f32[2,256,2,256]{3,1,2,0:T(8,128)}, u32[]{:S(2)}) copy-start(f32[2,256,2,256]{3,1,2,0:T(8,128)} %copy-done.3) | copy-start | bytes 3145732
  369.3 23.1 %collective-permute-start.23 = (f32[1,256,2,256]{3,1,2,0:T(8,128)}, f32[1,256,2,256]{3,1,2,0:T(8,128)}, u32[]{:S(2)}, u32[]{:S(2)}) collective-permute-start(f32[1,256,2,256]{3,1,2,0:T(8,128)} %slice.400), channel_id=1, source_target_pairs={{2,0},{4,2},{6,4},{8,6},{10,8},{12,10},{14,12},{16,14},{18,16},{20... | collective-permute-start | bytes 1572872 | tf_op jit(solution)/shard_map/ppermute | solution.py:20
  378.9 10.1 %all-to-all-start.5 = ((bf16[2,128,1024]{2,1,0:T(8,128)(2,1)}), bf16[2,128,1024]{2,1,0:T(8,128)(2,1)S(1)}, u32[]{:S(2)}, u32[]{:S(2)}) async-start(bf16[2,128,1024]{2,1,0:T(8,128)(2,1)} %convert_element_type.84), calls=%async_computation.5 | async-start | bytes 1048576 | tf_op jit(solution)/shard_map/all_to_all | solution.py:170
  389.0 8.6 %all-to-all-start.6 = ((bf16[2,128,512]{2,1,0:T(8,128)(2,1)}), bf16[2,128,512]{2,1,0:T(8,128)(2,1)S(1)}, u32[]{:S(2)}, u32[]{:S(2)}) async-start(bf16[2,128,512]{2,1,0:T(8,128)(2,1)} %convert_element_type.85), calls=%async_computation.6 | async-start | bytes 524288 | tf_op jit(solution)/shard_map/all_to_all | solution.py:177
  397.6 8.6 %all-to-all-start.7 = ((bf16[2,128,512]{2,1,0:T(8,128)(2,1)}), bf16[2,128,512]{2,1,0:T(8,128)(2,1)S(1)}, u32[]{:S(2)}, u32[]{:S(2)}) async-start(bf16[2,128,512]{2,1,0:T(8,128)(2,1)} %convert_element_type.87), calls=%async_computation.7 | async-start | bytes 524288 | tf_op jit(solution)/shard_map/all_to_all | solution.py:180
where the time goes:
time: 410 us; the launch traced here: 407 us
  waiting for transfers between devices  142 us (35%)
  starting transfers between devices  101 us (25%)
  local copies, waits for them, and re-layouts  81.1 us (20%)
  matrix products  41.9 us (10%)
  other arithmetic  36.4 us (9%)
  between operations  4.61 us (1%)
    ppermute x24, waiting for transfers between devices, from_behind(): return lax.ppermute(block, axis, route)  122 us
    ppermute x24, starting transfers between devices, from_behind(): return lax.ppermute(block, axis, route)  72.5 us
    unnamed x60, local copies, waits for them, and re-layouts  26.8 us
    dot_general x1, matrix products, attend(): jnp.einsum('kgtu,ukd->tkgd', grad_score, key_all, preferred_element_type=...  11.7 us
    dot_general x1, matrix products, attend(): jnp.einsum('kgtu,tkgd->ukd', grad_score, query, preferred_element_type=jn...  11 us
  transfers between devices with their start and end apart: 32, of which 12 were waited for; matrix products, arithmetic and copies ran while one was open for 28% of the time, Pallas kernels for 0%

commit v1 on v0

v1 whole, which is shorter than its diff:
```python
import functools
import math

import jax
import jax.numpy as jnp
from jax import lax
from jax.experimental import pallas as pl
from jax.experimental.pallas import tpu as pltpu
from jax.sharding import PartitionSpec as P

HD = 256
GROUP = 2
WINDOW = 1024
FORK = 2
BASE = 10000.0
SLOTS = 9
VMEM_LIMIT = 48 * 2**20
MESH = pl.DeviceIdType.MESH


def tree_tables(parent_gap, own_shard, levels):
    count = parent_gap.shape[0]
    ordinal = jnp.arange(count, dtype=jnp.int32)
    deeper = (parent_gap == 1).astype(jnp.int32)
    depths = jnp.sum(jnp.where(ordinal[None, :] <= ordinal[:, None], deeper[None, :], 0), 1)
    depth = jnp.sum(jnp.where(ordinal <= own_shard, deeper, 0))
    height = jnp.arange(levels + 1, dtype=jnp.int32)
    match = jnp.logical_and(
        depths[None, :] == depth - height[:, None], ordinal[None, :] <= own_shard
    )
    elder = jnp.max(jnp.where(match, ordinal[None, :], -1), 1)
    present = elder >= 0
    slot = jnp.where(present, own_shard - elder, 0)
    return depth, slot.astype(jnp.int32), present.astype(jnp.int32)


def angles(depth, tokens):
    half = HD // 2
    position = depth * tokens + jnp.arange(tokens, dtype=jnp.int32)
    frequency = jnp.exp(jnp.arange(half, dtype=jnp.float32) * (-2.0 * math.log(BASE) / HD))
    angle = position.astype(jnp.float32)[:, None] * frequency[None, :]
    return jnp.cos(angle), jnp.sin(angle)


def turn(block, cosine, sine):
    half = HD // 2
    first, second = block[:, :half], block[:, half:]
    return jnp.concatenate([first * cosine - second * sine, second * cosine + first * sine], -1)


def greet(shards, heads):
    me, head = lax.axis_index("ctx"), lax.axis_index("head")
    core, row = lax.rem(me, 2), lax.rem(me // 2, 2)
    barrier = pltpu.get_barrier_semaphore()
    up, down = me + 4 < shards, me >= 4
    for step in range(1, heads):
        pl.semaphore_signal(
            barrier, inc=1, device_id={"head": lax.rem(head + step, heads)}, device_id_type=MESH
        )
    for other in (me + 1 - 2 * core, me + 2 - 4 * row):
        pl.semaphore_signal(barrier, inc=1, device_id={"ctx": other}, device_id_type=MESH)

    @pl.when(up)
    def _():
        pl.semaphore_signal(barrier, inc=1, device_id={"ctx": me + 4}, device_id_type=MESH)

    @pl.when(down)
    def _():
        pl.semaphore_signal(barrier, inc=1, device_id={"ctx": me - 4}, device_id_type=MESH)

    pl.semaphore_wait(barrier, heads + 1 + up.astype(jnp.int32) + down.astype(jnp.int32))
    return me, head, core, row


def both(*terms):
    return functools.reduce(jnp.logical_and, terms)


def remote(src, dst, send_sem, recv_sem, device):
    return pltpu.make_async_remote_copy(
        src_ref=src,
        dst_ref=dst,
        send_sem=send_sem,
        recv_sem=recv_sem,
        device_id=device,
        device_id_type=MESH,
    )


def gather_kernel(
    shards, heads, q, k, v, g, cosine, sine, qh, gh, kb, vb,
    qr, kr, y_send, y_recv, y_local, c_send, c_recv,
):
    me, head, core, row = greet(shards, heads)
    rows = q.shape[0]
    mine = pl.ds(pl.multiple_of(head * rows, rows), rows)
    cos, sin = cosine[mine, :], sine[mine, :]

    def rotate(src, dst):
        for i in range(src.shape[1] // HD):
            at = slice(i * HD, (i + 1) * HD)
            dst[:, at] = turn(src[:, at].astype(jnp.float32), cos, sin).astype(jnp.bfloat16)

    exchanged = {}

    def exchange(index, src, dst):
        width = src.shape[1] // heads
        copies = []
        for step in range(1, heads):
            peer = lax.rem(head + step, heads)
            columns = pl.ds(pl.multiple_of(peer * width, width), width)
            copies.append(
                remote(
                    src.at[:, columns], dst.at[mine, :],
                    y_send.at[index, step - 1], y_recv.at[index, step - 1], {"head": peer},
                )
            )
        columns = pl.ds(pl.multiple_of(head * width, width), width)
        local = pltpu.make_async_copy(src.at[:, columns], dst.at[mine, :], y_local.at[index])
        for copy in copies:
            copy.start()
        local.start()
        exchanged[index] = (copies, local)

    def arrived(index):
        copies, local = exchanged[index]
        local.wait()
        for copy in copies:
            copy.wait_recv()

    buffers = (kb, vb)
    sends = []

    def send(kv, src, dst, target, *conditions):
        copy = remote(
            buffers[kv].at[src], buffers[kv].at[dst],
            c_send.at[len(sends)], c_recv.at[kv, dst], {"ctx": target},
        )
        condition = both(me >= src, *conditions)
        pl.when(condition)(copy.start)
        sends.append((condition, copy))

    def received(kv, slot):
        copy = remote(
            buffers[kv].at[slot], buffers[kv].at[slot],
            c_send.at[0], c_recv.at[kv, slot], {"ctx": me + 1 - 2 * core},
        )
        pl.when(me >= slot)(copy.wait_recv)

    rotate(k, kr)
    exchange(0, kr, kb.at[0])
    exchange(1, v, vb.at[0])
    rotate(q, qr)
    up = me + 4 < shards
    for kv in (0, 1):
        arrived(kv)
        send(kv, 0, 4, me + 4, up)
        send(kv, 0, 2, me + 2, row == 0)
        send(kv, 0, 1, me + 1, core == 0)
    exchange(2, qr, qh)
    exchange(3, g, gh)
    for kv in (0, 1):
        received(kv, 4)
        send(kv, 4, 8, me + 4, up)
        send(kv, 4, 6, me + 2, row == 0)
        send(kv, 4, 2, me - 2, row == 1)
        send(kv, 4, 5, me + 1, core == 0)
        send(kv, 4, 3, me - 1, core == 1)
    for kv in (0, 1):
        received(kv, 2)
        send(kv, 2, 3, me + 1, core == 0)
        send(kv, 2, 1, me - 1, core == 1)
    for kv in (0, 1):
        received(kv, 8)
        send(kv, 8, 6, me - 2, row == 1)
        send(kv, 8, 7, me - 1, core == 1)
    for kv in (0, 1):
        received(kv, 6)
        send(kv, 6, 7, me + 1, core == 0)
        send(kv, 6, 5, me - 1, core == 1)
    arrived(2)
    arrived(3)
    for slot in (1, 3, 5, 7):
        for kv in (0, 1):
            received(kv, slot)
    for condition, copy in sends:
        pl.when(condition)(copy.wait_send)
    for copies, _ in exchanged.values():
        for copy in copies:
            copy.wait_send()


def gather(shards, heads, q, k, v, g, cosine, sine):
    rows = q.shape[0]
    tokens = rows * heads
    wide, narrow = q.shape[1] // heads, k.shape[1] // heads
    vmem = pl.BlockSpec(memory_space=pltpu.VMEM)
    hbm = pl.BlockSpec(memory_space=pl.ANY)
    low = jnp.bfloat16
    return pl.pallas_call(
        functools.partial(gather_kernel, shards, heads),
        out_shape=[
            jax.ShapeDtypeStruct((tokens, wide), low),
            jax.ShapeDtypeStruct((tokens, wide), low),
            jax.ShapeDtypeStruct((SLOTS, tokens, narrow), low),
            jax.ShapeDtypeStruct((SLOTS, tokens, narrow), low),
        ],
        in_specs=[vmem] * 6,
        out_specs=[hbm] * 4,
        scratch_shapes=[
            pltpu.VMEM(q.shape, low),
            pltpu.VMEM(k.shape, low),
            pltpu.SemaphoreType.DMA((4, heads - 1)),
            pltpu.SemaphoreType.DMA((4, heads - 1)),
            pltpu.SemaphoreType.DMA((4,)),
            pltpu.SemaphoreType.DMA((28,)),
            pltpu.SemaphoreType.DMA((2, SLOTS)),
        ],
        compiler_params=pltpu.CompilerParams(
            collective_id=0, has_side_effects=True, vmem_limit_bytes=VMEM_LIMIT
        ),
        name="gather",
    )(q, k, v, g, cosine, sine)


def attend_kernel(levels, table, *refs):
    q, g = refs[:2]
    keys, values = refs[2 : 3 + levels], refs[3 + levels : 4 + 2 * levels]
    cosine, sine, out, grad_q, part_k, part_v = refs[4 + 2 * levels :]
    tokens = q.shape[0]
    scaling = HD**-0.5
    f32, low = jnp.float32, jnp.bfloat16
    query = jnp.concatenate([q[:, i * HD : (i + 1) * HD] for i in range(GROUP)], 0)
    grad = jnp.concatenate([g[:, i * HD : (i + 1) * HD] for i in range(GROUP)], 0)
    across = (((1,), (1,)), ((), ()))
    down = (((0,), (0,)), ((), ()))
    key_at = lax.broadcasted_iota(jnp.int32, (tokens, tokens), 1)
    query_at = lax.broadcasted_iota(jnp.int32, (tokens, tokens), 0)
    later = jnp.concatenate([(key_at - query_at).astype(f32)] * GROUP, 0) > 0
    scores = []
    for j in range(levels + 1):
        s = lax.dot_general(query, keys[j][0], across, preferred_element_type=f32) * scaling
        if j == 0:
            s = jnp.where(later, -1e30, s)
        else:
            if j == levels:
                s = jnp.where(later, s, -1e30)
            s = jnp.where(table[levels + 1 + j] > 0, s, -1e30)
        scores.append(s)
    highest = functools.reduce(jnp.maximum, [jnp.max(s, -1, keepdims=True) for s in scores])
    raw = [jnp.exp(s - highest) for s in scores]
    total = sum(jnp.sum(r, -1, keepdims=True) for r in raw)
    inverse = 1.0 / total
    probs = [r * inverse for r in raw]
    probs_low = [p.astype(low) for p in probs]
    attended = sum(
        lax.dot(p, values[j][0], preferred_element_type=f32) for j, p in enumerate(probs_low)
    )
    grad_probs = [
        lax.dot_general(grad, values[j][0], across, preferred_element_type=f32)
        for j in range(levels + 1)
    ]
    delta = sum(jnp.sum(p * d, -1, keepdims=True) for p, d in zip(probs, grad_probs))
    grad_scores = [
        (p * (d - delta) * scaling).astype(low) for p, d in zip(probs, grad_probs)
    ]
    turned = sum(
        lax.dot(d, keys[j][0], preferred_element_type=f32) for j, d in enumerate(grad_scores)
    )
    cos, sin = cosine[...], -sine[...]
    for i in range(GROUP):
        rows, at = slice(i * tokens, (i + 1) * tokens), slice(i * HD, (i + 1) * HD)
        out[:, at] = attended[rows].astype(low)
        grad_q[:, at] = turn(turned[rows], cos, sin).astype(low)
    part_k[...] = jnp.zeros_like(part_k)
    part_v[...] = jnp.zeros_like(part_v)
    for j in range(levels + 1):

        def put(j=j):
            slot = table[j]
            part_k[slot] = lax.dot_general(
                grad_scores[j], query, down, preferred_element_type=f32
            ).astype(low)
            part_v[slot] = lax.dot_general(
                probs_low[j], grad, down, preferred_element_type=f32
            ).astype(low)

        pl.when(table[levels + 1 + j] > 0)(put)


def attend(levels, table, qh, gh, kb, vb, cosine, sine):
    tokens = qh.shape[0]
    kv_local = kb.shape[2] // HD
    low = jnp.bfloat16

    def chosen(j):
        return pl.BlockSpec((1, tokens, HD), lambda h, t: (t[j], 0, h))

    wide = pl.BlockSpec((tokens, GROUP * HD), lambda h, t: (0, h))
    table_spec = pl.BlockSpec((tokens, HD // 2), lambda h, t: (0, 0))
    part = pl.BlockSpec((SLOTS, tokens, HD), lambda h, t: (0, 0, h))
    count = levels + 1
    return pl.pallas_call(
        functools.partial(attend_kernel, levels),
        out_shape=[
            jax.ShapeDtypeStruct(qh.shape, low),
            jax.ShapeDtypeStruct(qh.shape, low),
            jax.ShapeDtypeStruct(kb.shape, low),
            jax.ShapeDtypeStruct(vb.shape, low),
        ],
        grid_spec=pltpu.PrefetchScalarGridSpec(
            num_scalar_prefetch=1,
            grid=(kv_local,),
            in_specs=[wide, wide]
            + [chosen(j) for j in range(count)] * 2
            + [table_spec, table_spec],
            out_specs=[wide, wide, part, part],
        ),
        compiler_params=pltpu.CompilerParams(vmem_limit_bytes=VMEM_LIMIT),
        name="attend",
    )(table, qh, gh, *[kb] * count, *[vb] * count, cosine, sine)


def return_kernel(
    shards, heads, out, grad_q, part_k, part_v, cosine, sine, out_o, out_q, out_k, out_v,
    acc, from_core, from_row, from_up, done, y_send, y_recv, y_local, c_send, c_recv,
):
    me, head, core, row = greet(shards, heads)
    rows = out_o.shape[0]
    f32, low = jnp.float32, jnp.bfloat16
    exchanged = []

    def exchange(src, dst):
        index = len(exchanged)
        width = src.shape[1]
        columns = pl.ds(pl.multiple_of(head * width, width), width)
        copies = []
        for step in range(1, heads):
            peer = lax.rem(head + step, heads)
            theirs = pl.ds(pl.multiple_of(peer * rows, rows), rows)
            copies.append(
                remote(
                    src.at[theirs, :], dst.at[:, columns],
                    y_send.at[index, step - 1], y_recv.at[index, step - 1], {"head": peer},
                )
            )
        mine = pl.ds(pl.multiple_of(head * rows, rows), rows)
        local = pltpu.make_async_copy(src.at[mine, :], dst.at[:, columns], y_local.at[index])
        for copy in copies:
            copy.start()
        local.start()
        exchanged.append((copies, local))

    parts = (part_k, part_v)
    core_copies, row_copies, up_copies = {}, {}, {}
    for i in (3, 2, 1, 0):
        for kv in (0, 1):
            core_copies[kv, i] = remote(
                parts[kv].at[2 * i + 1], from_core.at[kv, i],
                c_send.at[kv, i], c_recv.at[kv, i], {"ctx": me + 1 - 2 * core},
            )
            core_copies[kv, i].start()

    def to_row(kv, i, slot):
        row_copies[kv, i] = remote(
            acc.at[kv, slot // 2], from_row.at[kv, i],
            c_send.at[kv, 4 + i], c_recv.at[kv, 4 + i], {"ctx": me + 2 - 4 * row},
        )
        row_copies[kv, i].start()

    has_down, has_up = me >= 4, me + 4 < shards

    def to_down(kv, i, slot):
        up_copies[kv, i] = remote(
            acc.at[kv, slot // 2], from_up.at[kv, i],
            c_send.at[kv, 6 + i], c_recv.at[kv, 6 + i], {"ctx": me - 4},
        )
        pl.when(has_down)(up_copies[kv, i].start)

    def add(kv, slot, piece):
        at = slot // 2
        acc[kv, at] = (acc[kv, at].astype(f32) + piece.astype(f32)).astype(low)

    def start(kv, slot, piece):
        acc[kv, slot // 2] = (parts[kv][slot].astype(f32) + piece.astype(f32)).astype(low)

    for kv in (0, 1):
        core_copies[kv, 3].wait_recv()
        core_copies[kv, 2].wait_recv()
        start(kv, 6, from_core[kv, 3 - core])
        to_row(kv, 1, 6)
    for kv in (0, 1):

        @pl.when(core == 1)
        def _(kv=kv):
            start(kv, 8, from_core[kv, 3])

        @pl.when(core == 0)
        def _(kv=kv):
            acc[kv, 4] = parts[kv][8]

        core_copies[kv, 1].wait_recv()
        core_copies[kv, 0].wait_recv()
        start(kv, 2, from_core[kv, 1 - core])
        to_row(kv, 0, 2)
    exchange(out, out_o)
    exchange(grad_q, out_q)
    for kv in (0, 1):
        start(kv, 4, from_core[kv, 2 - core])

        @pl.when(core == 0)
        def _(kv=kv):
            start(kv, 0, from_core[kv, 0])

        @pl.when(core == 1)
        def _(kv=kv):
            acc[kv, 0] = parts[kv][0]

    for kv in (0, 1):
        row_copies[kv, 1].wait_recv()

        @pl.when(row == 1)
        def _(kv=kv):
            add(kv, 8, from_row[kv, 1])

        @pl.when(row == 0)
        def _(kv=kv):
            add(kv, 4, from_row[kv, 1])

        to_down(kv, 1, 8)
    for kv in (0, 1):
        row_copies[kv, 0].wait_recv()

        @pl.when(row == 1)
        def _(kv=kv):
            add(kv, 4, from_row[kv, 0])

        @pl.when(row == 0)
        def _(kv=kv):
            add(kv, 0, from_row[kv, 0])

        @pl.when(has_up)
        def _(kv=kv):
            up_copies[kv, 1].wait_recv()
            add(kv, 4, from_up[kv, 1])

        to_down(kv, 0, 4)
    for kv in (0, 1):

        @pl.when(has_up)
        def _(kv=kv):
            up_copies[kv, 0].wait_recv()
            add(kv, 0, from_up[kv, 0])

        if kv == 0:
            cos, sin = cosine[...], -sine[...]
            for i in range(acc.shape[3] // HD):
                at = slice(i * HD, (i + 1) * HD)
                done[kv, :, at] = turn(acc[kv, 0, :, at].astype(f32), cos, sin).astype(low)
        else:
            done[kv] = acc[kv, 0]
        exchange(done.at[kv], (out_k, out_v)[kv])
    for copies, local in exchanged:
        for copy in copies:
            copy.wait()
        local.wait()
    for copies in (core_copies, row_copies):
        for copy in copies.values():
            copy.wait_send()
    for copy in up_copies.values():
        pl.when(has_down)(copy.wait_send)


def give_back(shards, heads, out, grad_q, part_k, part_v, cosine, sine):
    tokens, narrow = part_k.shape[1:]
    rows = tokens // heads
    low = jnp.bfloat16
    vmem = pl.BlockSpec(memory_space=pltpu.VMEM)
    hbm = pl.BlockSpec(memory_space=pl.ANY)
    wide_out = jax.ShapeDtypeStruct((rows, out.shape[1] * heads), low)
    narrow_out = jax.ShapeDtypeStruct((rows, narrow * heads), low)
    return pl.pallas_call(
        functools.partial(return_kernel, shards, heads),
        out_shape=[wide_out, wide_out, narrow_out, narrow_out],
        in_specs=[hbm, hbm, vmem, vmem, vmem, vmem],
        out_specs=[hbm] * 4,
        scratch_shapes=[
            pltpu.VMEM((2, 5, tokens, narrow), low),
            pltpu.VMEM((2, 4, tokens, narrow), low),
            pltpu.VMEM((2, 2, tokens, narrow), low),
            pltpu.VMEM((2, 2, tokens, narrow), low),
            pltpu.VMEM((2, tokens, narrow), low),
            pltpu.SemaphoreType.DMA((4, heads - 1)),
            pltpu.SemaphoreType.DMA((4, heads - 1)),
            pltpu.SemaphoreType.DMA((4,)),
            pltpu.SemaphoreType.DMA((2, 8)),
            pltpu.SemaphoreType.DMA((2, 8)),
        ],
        compiler_params=pltpu.CompilerParams(
            collective_id=1, has_side_effects=True, vmem_limit_bytes=VMEM_LIMIT
        ),
        name="give_back",
    )(out, grad_q, part_k, part_v, cosine, sine)


def run(shards, heads, queries, keys, values, grad_attn, parent_gap):
    tokens = queries.shape[0] * heads
    levels = WINDOW // tokens
    assert levels * FORK == SLOTS - 1 and shards % 4 == 0
    own_shard = lax.axis_index("ctx")
    depth, slot, present = tree_tables(parent_gap, own_shard, levels)
    cosine, sine = angles(depth, tokens)
    table = jnp.concatenate([slot, present])
    qh, gh, kb, vb = gather(
        shards, heads, queries, keys, values, grad_attn, cosine, sine
    )
    out, grad_q, part_k, part_v = attend(levels, table, qh, gh, kb, vb, cosine, sine)
    return tuple(give_back(shards, heads, out, grad_q, part_k, part_v, cosine, sine))


def solution(mesh):
    rows = P(("ctx", "head"), None)
    return jax.shard_map(
        functools.partial(run, mesh.shape["ctx"], mesh.shape["head"]),
        mesh=mesh,
        in_specs=(rows, rows, rows, rows, P()),
        out_specs=(rows, rows, rows, rows),
        check_vma=False,
    )
```

time: 410 us -> 108 us (0.26)
  the two profiles are of different devices: /device:TPU:24 before, /device:TPU:0 now
where the time goes in v1:
time: 108 us; the launch traced here: 107 us
  Pallas kernels  93.5 us (87%)
  local copies, waits for them, and re-layouts  8.36 us (8%)
  other arithmetic  3.55 us (3%)
  between operations  1.36 us (1%)
    pallas_call x1, Pallas kernels, give_back(): pl.pallas_call(functools.partial(return_kernel, shards, heads), out_shape...  60.5 us
    pallas_call x1, Pallas kernels, gather(): pl.pallas_call(functools.partial(gather_kernel, shards, heads), out_shape...  22.8 us
    pallas_call x1, Pallas kernels, attend(): pl.pallas_call(functools.partial(attend_kernel, levels), out_shape=[jax.S...  10.2 us
    unnamed x14, local copies, waits for them, and re-layouts  8.36 us

profile of v1, /device:TPU:0, one launch (start us, length us, event | category | flops | bytes accessed | tf_op | source)
XLA Modules:
  0.0 106.8 jit_solution(3679899138982802636)
XLA Ops:
  0.6 1.3 %select_reduce_fusion.2 = s32[]{:T(128)} fusion(s32[16]{0:T(128)} %param.9, s32[]{:T(128)S(6)} %axis_index.15), kind=kLoop, calls=%fused_computation.12 | loop fusion | flops 79 | bytes 72 | tf_op jit(solution)/shard_map/reduce_sum | solution.py:26
  2.6 0.6 iota_subtract_fusion
  3.3 0.7 compare_convert_fusion
  3.9 0.1 select_reduce_fusion
  4.0 0.2 select_reduce_fusion.1
  4.2 0.1 pad_add_fusion.table
  4.3 0.5 multiply_sine_fusion
  4.9 0.0 copy-start.1
  4.9 1.0 copy-done.1
  5.9 0.0 copy-start.2
  5.9 1.0 copy-done.2
  7.0 0.0 copy-start.3
  7.0 0.9 copy-done.3
  7.9 0.0 copy-start.4
  7.9 0.9 copy-done.4
  8.9 22.8 %gather.1 = (bf16[256,1024]{1,0:T(8,128)(2,1)S(1)}, bf16[256,1024]{1,0:T(8,128)(2,1)S(1)}, bf16[9,256,512]{2,1,0:T(8,128)(2,1)S(1)}, bf16[9,256,512]{2,1,0:T(8,128)(2,1)}) custom-call(bf16[128,2048]{1,0:T(8,128)(2,1)S(1)} %copy-done.1, bf16[128,1024]{1,0:T(8,128)(2,1)S(1)} %copy-done.3, bf16[128,1024]{1,0:T(8,128)(2,1)S(1)} %copy-done.4, ...), custom_call_target="tpu_custom_call" | custom-call | tf_op jit(solution)/shard_map/gather/pallas_call | solution.py:200
  31.7 0.0 copy-start
  31.7 1.4 %copy-done = bf16[9,256,512]{2,1,0:T(8,128)(2,1)} copy-done((bf16[9,256,512]{2,1,0:T(8,128)(2,1)}, bf16[9,256,512]{2,1,0:T(8,128)(2,1)S(1)}, u32[]{:S(2)}) %copy-start) | copy-done | bytes 2359320
  33.1 10.2 %attend.1 = (bf16[256,1024]{1,0:T(8,128)(2,1)S(1)}, bf16[256,1024]{1,0:T(8,128)(2,1)S(1)}, bf16[9,256,512]{2,1,0:T(8,128)(2,1)S(1)}, bf16[9,256,512]{2,1,0:T(8,128)(2,1)}) custom-call(s32[10]{0:T(128)S(1)} %pad_add_fusion.table, bf16[256,1024]{1,0:T(8,128)(2,1)S(1)} %get-tuple-element.12.refs_0_, bf16[256,1024]{1,0:T(8,128)(2,1)S(1)} %get-tuple-element.13.refs_1_, ...), custom_call_target="tpu_custom_call" | custom-call | tf_op jit(solution)/shard_map/attend/pallas_call | solution.py:303
  43.3 60.5 %give_back.1 = (bf16[128,2048]{1,0:T(8,128)(2,1)S(1)}, bf16[128,2048]{1,0:T(8,128)(2,1)S(1)}, bf16[128,1024]{1,0:T(8,128)(2,1)S(1)}, bf16[128,1024]{1,0:T(8,128)(2,1)S(1)}) custom-call(bf16[256,1024]{1,0:T(8,128)(2,1)S(1)} %get-tuple-element.16.out, bf16[256,1024]{1,0:T(8,128)(2,1)S(1)} %get-tuple-element.17.grad_q, ...), custom_call_target="tpu_custom_call" | custom-call | tf_op jit(solution)/shard_map/give_back/pallas_call | solution.py:482
  103.8 0.8 copy.13
  104.6 0.8 copy.14
  105.4 0.7 copy.15
  106.1 0.7 copy.16
  (5 shorter events, 0.0 us)
Async XLA Ops:
  4.9 1.0 copy-start.1
  5.9 1.0 copy-start.2
  7.0 0.9 copy-start.3
  7.9 0.9 copy-start.4
  31.7 1.4 %copy-start = (bf16[9,256,512]{2,1,0:T(8,128)(2,1)}, bf16[9,256,512]{2,1,0:T(8,128)(2,1)S(1)}, u32[]{:S(2)}) copy-start(bf16[9,256,512]{2,1,0:T(8,128)(2,1)S(1)} %get-tuple-element.14.refs_2_.refs_3_.refs_4_.refs_5_.refs_6_) | copy-start | bytes 7077892

commit v2 on v1

v2 whole, which is shorter than its diff:
```python
import functools
import math

import jax
import jax.numpy as jnp
from jax import lax
from jax.experimental import pallas as pl
from jax.experimental.pallas import tpu as pltpu
from jax.sharding import PartitionSpec as P

HD = 256
GROUP = 2
WINDOW = 1024
FORK = 2
BASE = 10000.0
SLOTS = 9
VMEM_LIMIT = 60 * 2**20
MESH = pl.DeviceIdType.MESH


def turn(block, cosine, sine):
    half = HD // 2
    first, second = block[:, :half], block[:, half:]
    return jnp.concatenate([first * cosine - second * sine, second * cosine + first * sine], -1)


def greet(shards, heads):
    me, head = lax.axis_index("ctx"), lax.axis_index("head")
    core, row = lax.rem(me, 2), lax.rem(me // 2, 2)
    barrier = pltpu.get_barrier_semaphore()
    up, down = me + 4 < shards, me >= 4
    for step in range(1, heads):
        pl.semaphore_signal(
            barrier, inc=1, device_id={"head": lax.rem(head + step, heads)}, device_id_type=MESH
        )
    for other in (me + 1 - 2 * core, me + 2 - 4 * row):
        pl.semaphore_signal(barrier, inc=1, device_id={"ctx": other}, device_id_type=MESH)

    @pl.when(up)
    def _():
        pl.semaphore_signal(barrier, inc=1, device_id={"ctx": me + 4}, device_id_type=MESH)

    @pl.when(down)
    def _():
        pl.semaphore_signal(barrier, inc=1, device_id={"ctx": me - 4}, device_id_type=MESH)

    pl.semaphore_wait(barrier, heads + 1 + up.astype(jnp.int32) + down.astype(jnp.int32))
    return me, head, core, row


def both(*terms):
    return functools.reduce(jnp.logical_and, terms)


def remote(src, dst, send_sem, recv_sem, device):
    return pltpu.make_async_remote_copy(
        src_ref=src,
        dst_ref=dst,
        send_sem=send_sem,
        recv_sem=recv_sem,
        device_id=device,
        device_id_type=MESH,
    )


def gather_kernel(
    shards, heads, levels, gap, q, k, v, g, qh, gh, kb, vb, table, cosine, sine,
    qi, ki, qr, kr, i_sem, y_send, y_recv, y_local, c_send, c_recv,
):
    load_k = pltpu.make_async_copy(k, ki, i_sem.at[0])
    load_q = pltpu.make_async_copy(q, qi, i_sem.at[1])
    load_k.start()
    load_q.start()
    me, head, core, row = greet(shards, heads)
    rows = q.shape[0]
    tokens = rows * heads

    def group(step):
        return pl.ds(pl.multiple_of(lax.rem(head + step, heads) * rows, rows), rows)

    def own_columns(src):
        width = src.shape[1] // heads
        return src.at[:, pl.ds(pl.multiple_of(head * width, width), width)]

    mine = group(0)
    exchanged = {}

    def exchange(index, src, dst):
        width = src.shape[1] // heads
        copies = []
        for step in range(1, heads):
            peer = lax.rem(head + step, heads)
            columns = pl.ds(pl.multiple_of(peer * width, width), width)
            copies.append(
                remote(
                    src.at[:, columns], dst.at[mine, :],
                    y_send.at[index, step - 1], y_recv.at[index, step - 1], {"head": peer},
                )
            )
        local = pltpu.make_async_copy(own_columns(src), dst.at[mine, :], y_local.at[index])
        for copy in copies:
            copy.start()
        local.start()
        exchanged[index] = (copies, local)

    buffers = (kb, vb)
    sends = []

    def send(chunk, src, dst, target, *conditions, source=None):
        kv, step = chunk
        at = group(step)
        copy = remote(
            buffers[kv].at[src, at, :] if source is None else own_columns(source),
            buffers[kv].at[dst, at, :],
            c_send.at[len(sends)], c_recv.at[kv, step, dst], {"ctx": target},
        )
        condition = both(me >= src, *conditions)
        pl.when(condition)(copy.start)
        sends.append((condition, copy))

    def received(chunk, slot):
        kv, step = chunk
        place = buffers[kv].at[slot, group(step), :]
        copy = remote(
            place, place, c_send.at[0], c_recv.at[kv, step, slot], {"ctx": me + 1 - 2 * core}
        )
        pl.when(me >= slot)(copy.wait_recv)

    up = me + 4 < shards

    def first(chunk, source=None):
        send(chunk, 0, 4, me + 4, up, source=source)
        send(chunk, 0, 2, me + 2, row == 0, source=source)
        send(chunk, 0, 1, me + 1, core == 0, source=source)

    first((1, 0), v)
    exchange(1, v, vb.at[0])

    def count(i, depth):
        return depth + jnp.where(jnp.logical_and(i <= me, gap[i] == 1), 1, 0)

    depth = lax.fori_loop(0, shards, count, jnp.int32(0))
    height = jnp.int32(0)
    slots = [jnp.int32(0)] * (levels + 1)
    for offset in range(1, SLOTS):
        height = height + jnp.where(gap[jnp.maximum(me - offset + 1, 0)] == 1, 1, 0)
        for j in range(1, levels + 1):
            found = both(slots[j] == 0, height == j, me >= offset)
            slots[j] = jnp.where(found, offset, slots[j])
    for j in range(levels + 1):
        table[j] = slots[j]
        table[levels + 1 + j] = jnp.int32(1) if j == 0 else jnp.where(slots[j] > 0, 1, 0)

    half = HD // 2
    position = depth * tokens + lax.broadcasted_iota(jnp.int32, (tokens, half), 0)
    lane = lax.broadcasted_iota(jnp.int32, (tokens, half), 1).astype(jnp.float32)
    angle = position.astype(jnp.float32) * jnp.exp(lane * (-2.0 * math.log(BASE) / HD))
    cosine[...] = jnp.cos(angle)
    sine[...] = jnp.sin(angle)
    cos, sin = cosine[mine, :], sine[mine, :]

    def rotate(src, dst):
        for i in range(src.shape[1] // HD):
            at = slice(i * HD, (i + 1) * HD)
            dst[:, at] = turn(src[:, at].astype(jnp.float32), cos, sin).astype(jnp.bfloat16)

    load_k.wait()
    rotate(ki, kr)
    exchange(0, kr, kb.at[0])
    first((0, 0), kr)
    load_q.wait()
    rotate(qi, qr)
    for step in range(1, heads):
        for kv in (1, 0):
            exchanged[kv][0][heads - step - 1].wait_recv()
            first((kv, step))
    exchange(2, qr, qh)
    exchange(3, g, gh)

    def second(chunk):
        received(chunk, 4)
        send(chunk, 4, 8, me + 4, up)
        send(chunk, 4, 6, me + 2, row == 0)
        send(chunk, 4, 2, me - 2, row == 1)
        send(chunk, 4, 5, me + 1, core == 0)
        send(chunk, 4, 3, me - 1, core == 1)

    def across(chunk):
        received(chunk, 2)
        send(chunk, 2, 3, me + 1, core == 0)
        send(chunk, 2, 1, me - 1, core == 1)

    def third(chunk):
        received(chunk, 8)
        send(chunk, 8, 6, me - 2, row == 1)
        send(chunk, 8, 7, me - 1, core == 1)

    def last(chunk):
        received(chunk, 6)
        send(chunk, 6, 7, me + 1, core == 0)
        send(chunk, 6, 5, me - 1, core == 1)

    chunks = [(kv, step) for step in range(heads) for kv in (1, 0)]
    for ahead, behind in ((second, across), (third, last)):
        for chunk, before in zip(chunks + [None], [None] + chunks):
            if chunk is not None:
                ahead(chunk)
            if before is not None:
                behind(before)
    for index in range(4):
        copies, local = exchanged[index]
        local.wait()
        for copy in copies:
            copy.wait_send()
            if index > 1:
                copy.wait_recv()
    for slot in (1, 3, 5, 7):
        for chunk in chunks:
            received(chunk, slot)
    for condition, copy in sends:
        pl.when(condition)(copy.wait_send)


def gather(shards, heads, levels, gap, q, k, v, g):
    rows = q.shape[0]
    tokens = rows * heads
    wide, narrow = q.shape[1] // heads, k.shape[1] // heads
    vmem = pl.BlockSpec(memory_space=pltpu.VMEM)
    smem = pl.BlockSpec(memory_space=pltpu.SMEM)
    hbm = pl.BlockSpec(memory_space=pltpu.HBM)
    low = jnp.bfloat16
    angle = jax.ShapeDtypeStruct((tokens, HD // 2), jnp.float32)
    return pl.pallas_call(
        functools.partial(gather_kernel, shards, heads, levels),
        out_shape=[
            jax.ShapeDtypeStruct((tokens, wide), low),
            jax.ShapeDtypeStruct((tokens, wide), low),
            jax.ShapeDtypeStruct((SLOTS, tokens, narrow), low),
            jax.ShapeDtypeStruct((SLOTS, tokens, narrow), low),
            jax.ShapeDtypeStruct((2 * (levels + 1),), jnp.int32),
            angle,
            angle,
        ],
        in_specs=[smem] + [hbm] * 4,
        out_specs=[hbm] * 4 + [smem, vmem, vmem],
        scratch_shapes=[
            pltpu.VMEM(q.shape, low),
            pltpu.VMEM(k.shape, low),
            pltpu.VMEM(q.shape, low),
            pltpu.VMEM(k.shape, low),
            pltpu.SemaphoreType.DMA((2,)),
            pltpu.SemaphoreType.DMA((4, heads - 1)),
            pltpu.SemaphoreType.DMA((4, heads - 1)),
            pltpu.SemaphoreType.DMA((4,)),
            pltpu.SemaphoreType.DMA((28 * heads,)),
            pltpu.SemaphoreType.DMA((2, heads, SLOTS)),
        ],
        compiler_params=pltpu.CompilerParams(
            collective_id=0, has_side_effects=True, vmem_limit_bytes=VMEM_LIMIT
        ),
        name="gather",
    )(gap, q, k, v, g)


def attend_kernel(levels, table, *refs):
    q, g = refs[:2]
    keys, values = refs[2 : 3 + levels], refs[3 + levels : 4 + 2 * levels]
    cosine, sine, out, grad_q, part_k, part_v = refs[4 + 2 * levels :]
    tokens = q.shape[0]
    scaling = HD**-0.5
    f32, low = jnp.float32, jnp.bfloat16
    query = jnp.concatenate([q[:, i * HD : (i + 1) * HD] for i in range(GROUP)], 0)
    grad = jnp.concatenate([g[:, i * HD : (i + 1) * HD] for i in range(GROUP)], 0)
    across = (((1,), (1,)), ((), ()))
    down = (((0,), (0,)), ((), ()))
    key_at = lax.broadcasted_iota(jnp.int32, (tokens, tokens), 1)
    query_at = lax.broadcasted_iota(jnp.int32, (tokens, tokens), 0)
    later = jnp.concatenate([(key_at - query_at).astype(f32)] * GROUP, 0) > 0
    scores = []
    for j in range(levels + 1):
        s = lax.dot_general(query, keys[j][0], across, preferred_element_type=f32) * scaling
        if j == 0:
            s = jnp.where(later, -1e30, s)
        else:
            if j == levels:
                s = jnp.where(later, s, -1e30)
            s = jnp.where(table[levels + 1 + j] > 0, s, -1e30)
        scores.append(s)
    highest = functools.reduce(jnp.maximum, [jnp.max(s, -1, keepdims=True) for s in scores])
    raw = [jnp.exp(s - highest) for s in scores]
    total = sum(jnp.sum(r, -1, keepdims=True) for r in raw)
    inverse = 1.0 / total
    probs = [r * inverse for r in raw]
    probs_low = [p.astype(low) for p in probs]
    attended = sum(
        lax.dot(p, values[j][0], preferred_element_type=f32) for j, p in enumerate(probs_low)
    )
    grad_probs = [
        lax.dot_general(grad, values[j][0], across, preferred_element_type=f32)
        for j in range(levels + 1)
    ]
    delta = sum(jnp.sum(p * d, -1, keepdims=True) for p, d in zip(probs, grad_probs))
    grad_scores = [
        (p * (d - delta) * scaling).astype(low) for p, d in zip(probs, grad_probs)
    ]
    turned = sum(
        lax.dot(d, keys[j][0], preferred_element_type=f32) for j, d in enumerate(grad_scores)
    )
    cos, sin = cosine[...], -sine[...]
    for i in range(GROUP):
        rows, at = slice(i * tokens, (i + 1) * tokens), slice(i * HD, (i + 1) * HD)
        out[:, at] = attended[rows].astype(low)
        grad_q[:, at] = turn(turned[rows], cos, sin).astype(low)
    part_k[...] = jnp.zeros_like(part_k)
    part_v[...] = jnp.zeros_like(part_v)
    for j in range(levels + 1):

        def put(j=j):
            slot = table[j]
            part_k[slot] = lax.dot_general(
                grad_scores[j], query, down, preferred_element_type=f32
            ).astype(low)
            part_v[slot] = lax.dot_general(
                probs_low[j], grad, down, preferred_element_type=f32
            ).astype(low)

        pl.when(table[levels + 1 + j] > 0)(put)


def attend(levels, table, qh, gh, kb, vb, cosine, sine):
    tokens = qh.shape[0]
    kv_local = kb.shape[2] // HD
    low = jnp.bfloat16

    def chosen(j):
        return pl.BlockSpec((1, tokens, HD), lambda h, t: (t[j], 0, h))

    wide = pl.BlockSpec((tokens, GROUP * HD), lambda h, t: (0, h))
    table_spec = pl.BlockSpec((tokens, HD // 2), lambda h, t: (0, 0))
    part = pl.BlockSpec((SLOTS, tokens, HD), lambda h, t: (0, 0, h))
    count = levels + 1
    return pl.pallas_call(
        functools.partial(attend_kernel, levels),
        out_shape=[
            jax.ShapeDtypeStruct(qh.shape, low),
            jax.ShapeDtypeStruct(qh.shape, low),
            jax.ShapeDtypeStruct(kb.shape, low),
            jax.ShapeDtypeStruct(vb.shape, low),
        ],
        grid_spec=pltpu.PrefetchScalarGridSpec(
            num_scalar_prefetch=1,
            grid=(kv_local,),
            in_specs=[wide, wide]
            + [chosen(j) for j in range(count)] * 2
            + [table_spec, table_spec],
            out_specs=[wide, wide, part, part],
        ),
        compiler_params=pltpu.CompilerParams(vmem_limit_bytes=VMEM_LIMIT),
        name="attend",
    )(table, qh, gh, *[kb] * count, *[vb] * count, cosine, sine)


def return_kernel(
    shards, heads, out, grad_q, part_k, part_v, cosine, sine, out_o, out_q, out_k, out_v,
    acc, from_core, from_row, from_up, done, a_sem, y_send, y_recv, y_local,
    p_send, p_recv, p_local, c_send, c_recv,
):
    parts = (part_k, part_v)
    loads = {}
    for at in (3, 4, 1, 2, 0):
        for kv in (0, 1):
            loads[kv, at] = pltpu.make_async_copy(
                parts[kv].at[2 * at], acc.at[kv, at], a_sem.at[kv, at]
            )
            loads[kv, at].start()
    me, head, core, row = greet(shards, heads)
    rows = out_o.shape[0]
    f32, low = jnp.float32, jnp.bfloat16
    exchanged = []

    def group(step):
        return pl.ds(pl.multiple_of(lax.rem(head + 1 + step, heads) * rows, rows), rows)

    def exchange(src, dst):
        index = len(exchanged)
        width = src.shape[1]
        columns = pl.ds(pl.multiple_of(head * width, width), width)
        copies = []
        for step in range(1, heads):
            peer = lax.rem(head + step, heads)
            copies.append(
                remote(
                    src.at[group(step - 1), :], dst.at[:, columns],
                    y_send.at[index, step - 1], y_recv.at[index, step - 1], {"head": peer},
                )
            )
        local = pltpu.make_async_copy(
            src.at[group(heads - 1), :], dst.at[:, columns], y_local.at[index]
        )
        for copy in copies:
            copy.start()
        local.start()
        exchanged.append((copies, local))

    chunks = [(kv, step) for step in range(heads) for kv in (0, 1)]
    core_copies, row_copies, down_copies = {}, {}, {}
    for pair in ((3, 2), (1, 0)):
        for kv, step in chunks:
            at = group(step)
            for i in pair:
                core_copies[kv, step, i] = remote(
                    parts[kv].at[2 * i + 1, at, :], from_core.at[kv, i, at, :],
                    c_send.at[kv, step, i], c_recv.at[kv, step, i],
                    {"ctx": me + 1 - 2 * core},
                )
                core_copies[kv, step, i].start()

    def to_row(chunk, i, slot):
        kv, step = chunk
        at = group(step)
        row_copies[kv, step, i] = remote(
            acc.at[kv, slot // 2, at, :], from_row.at[kv, i, at, :],
            c_send.at[kv, step, 4 + i], c_recv.at[kv, step, 4 + i],
            {"ctx": me + 2 - 4 * row},
        )
        row_copies[kv, step, i].start()

    has_down, has_up = me >= 4, me + 4 < shards

    def to_down(chunk, i, slot):
        kv, step = chunk
        at = group(step)
        down_copies[kv, step, i] = remote(
            acc.at[kv, slot // 2, at, :], from_up.at[kv, i, at, :],
            c_send.at[kv, step, 6 + i], c_recv.at[kv, step, 6 + i], {"ctx": me - 4},
        )
        pl.when(has_down)(down_copies[kv, step, i].start)

    def add(chunk, slot, pieces, i):
        kv, step = chunk
        at = group(step)
        total = acc[kv, slot // 2, at, :].astype(f32) + pieces[kv, i, at, :].astype(f32)
        acc[kv, slot // 2, at, :] = total.astype(low)

    def add_when(condition, *args):
        pl.when(condition)(lambda: add(*args))

    for copy in loads.values():
        copy.wait()
    for chunk in chunks:
        core_copies[*chunk, 3].wait_recv()
        core_copies[*chunk, 2].wait_recv()
        add(chunk, 6, from_core, 3 - core)
        to_row(chunk, 1, 6)
        add_when(core == 1, chunk, 8, from_core, 3)
    exchange(out, out_o)
    exchange(grad_q, out_q)
    for chunk in chunks:
        core_copies[*chunk, 1].wait_recv()
        core_copies[*chunk, 0].wait_recv()
        add(chunk, 2, from_core, 1 - core)
        to_row(chunk, 0, 2)
        add(chunk, 4, from_core, 2 - core)
        add_when(core == 0, chunk, 0, from_core, 0)
    for chunk in chunks:
        row_copies[*chunk, 1].wait_recv()
        add_when(row == 1, chunk, 8, from_row, 1)
        to_down(chunk, 1, 8)
        add_when(row == 0, chunk, 4, from_row, 1)

    def middle(chunk):
        row_copies[*chunk, 0].wait_recv()
        add_when(row == 1, chunk, 4, from_row, 0)
        add_when(row == 0, chunk, 0, from_row, 0)

        @pl.when(has_up)
        def _():
            down_copies[*chunk, 1].wait_recv()
            add(chunk, 4, from_up, 1)

        to_down(chunk, 0, 4)

    finals = []

    def final(chunk):
        kv, step = chunk
        at = group(step)

        @pl.when(has_up)
        def _():
            down_copies[*chunk, 0].wait_recv()
            add(chunk, 0, from_up, 0)

        if kv == 0:
            cos, sin = cosine[at, :], -sine[at, :]
            for i in range(acc.shape[3] // HD):
                col = slice(i * HD, (i + 1) * HD)
                done[kv, at, col] = turn(acc[kv, 0, at, col].astype(f32), cos, sin).astype(low)
        else:
            done[kv, at, :] = acc[kv, 0, at, :]
        width = acc.shape[3]
        dst = (out_k, out_v)[kv].at[:, pl.ds(pl.multiple_of(head * width, width), width)]
        if step == heads - 1:
            copy = pltpu.make_async_copy(done.at[kv, at, :], dst, p_local.at[kv])
        else:
            copy = remote(
                done.at[kv, at, :], dst, p_send.at[kv, step], p_recv.at[kv, step],
                {"head": lax.rem(head + 1 + step, heads)},
            )
        copy.start()
        finals.append(copy)

    for chunk, before in zip(chunks + [None], [None] + chunks):
        if chunk is not None:
            middle(chunk)
        if before is not None:
            final(before)
    for copies, local in exchanged:
        for copy in copies:
            copy.wait()
        local.wait()
    for copies in (core_copies, row_copies):
        for copy in copies.values():
            copy.wait_send()
    for copy in down_copies.values():
        pl.when(has_down)(copy.wait_send)
    for copy in finals:
        copy.wait()


def give_back(shards, heads, out, grad_q, part_k, part_v, cosine, sine):
    tokens, narrow = part_k.shape[1:]
    rows = tokens // heads
    low = jnp.bfloat16
    vmem = pl.BlockSpec(memory_space=pltpu.VMEM)
    hbm = pl.BlockSpec(memory_space=pltpu.HBM)
    wide_out = jax.ShapeDtypeStruct((rows, out.shape[1] * heads), low)
    narrow_out = jax.ShapeDtypeStruct((rows, narrow * heads), low)
    peers = heads - 1
    return pl.pallas_call(
        functools.partial(return_kernel, shards, heads),
        out_shape=[wide_out, wide_out, narrow_out, narrow_out],
        in_specs=[hbm, hbm, hbm, hbm, vmem, vmem],
        out_specs=[pl.BlockSpec(memory_space=pl.ANY)] * 4,
        scratch_shapes=[
            pltpu.VMEM((2, 5, tokens, narrow), low),
            pltpu.VMEM((2, 4, tokens, narrow), low),
            pltpu.VMEM((2, 2, tokens, narrow), low),
            pltpu.VMEM((2, 2, tokens, narrow), low),
            pltpu.VMEM((2, tokens, narrow), low),
            pltpu.SemaphoreType.DMA((2, 5)),
            pltpu.SemaphoreType.DMA((2, peers)),
            pltpu.SemaphoreType.DMA((2, peers)),
            pltpu.SemaphoreType.DMA((2,)),
            pltpu.SemaphoreType.DMA((2, peers)),
            pltpu.SemaphoreType.DMA((2, peers)),
            pltpu.SemaphoreType.DMA((2,)),
            pltpu.SemaphoreType.DMA((2, heads, 8)),
            pltpu.SemaphoreType.DMA((2, heads, 8)),
        ],
        compiler_params=pltpu.CompilerParams(
            collective_id=1, has_side_effects=True, vmem_limit_bytes=VMEM_LIMIT
        ),
        name="give_back",
    )(out, grad_q, part_k, part_v, cosine, sine)


def settle_kernel(*refs):
    count = len(refs) // 2
    copies = [
        pltpu.make_async_copy(refs[i], refs[count + i], refs[-1].at[i]) for i in range(count)
    ]
    for copy in copies:
        copy.start()
    for copy in copies:
        copy.wait()


def settle(*arrays):
    space = pl.BlockSpec(memory_space=pl.ANY)
    return pl.pallas_call(
        settle_kernel,
        out_shape=[jax.ShapeDtypeStruct(a.shape, a.dtype) for a in arrays],
        in_specs=[space] * len(arrays),
        out_specs=[pl.BlockSpec(memory_space=pltpu.HBM)] * len(arrays),
        scratch_shapes=[pltpu.SemaphoreType.DMA((len(arrays),))],
        name="settle",
    )(*arrays)


def run(shards, heads, queries, keys, values, grad_attn, parent_gap):
    tokens = queries.shape[0] * heads
    levels = WINDOW // tokens
    assert levels * FORK == SLOTS - 1 and shards % 4 == 0
    qh, gh, kb, vb, table, cosine, sine = gather(
        shards, heads, levels, parent_gap, queries, keys, values, grad_attn
    )
    out, grad_q, part_k, part_v = attend(levels, table, qh, gh, kb, vb, cosine, sine)
    return tuple(settle(*give_back(shards, heads, out, grad_q, part_k, part_v, cosine, sine)))


def solution(mesh):
    rows = P(("ctx", "head"), None)
    return jax.shard_map(
        functools.partial(run, mesh.shape["ctx"], mesh.shape["head"]),
        mesh=mesh,
        in_specs=(rows, rows, rows, rows, P()),
        out_specs=(rows, rows, rows, rows),
        check_vma=False,
    )
```

time: 108 us -> 136 us (1.26)
  Pallas kernels: 93.5 us -> 135 us
  local copies, waits for them, and re-layouts: 8.36 us -> 0 us
  other arithmetic: 3.55 us -> 0 us
    pallas_call x1 -> x2, Pallas kernels: 22.8 us -> 73.8 us  [the longest x1 48.8 us: settle(): pl.pallas_call(settle_kernel, out_shape=[jax.ShapeDtypeStruct(a.shape, a....]
    pallas_call x1, Pallas kernels: 60.5 us -> 50.1 us  [give_back(): pl.pallas_call(functools.partial(return_kernel, shards, heads), out_shape...]
    unnamed x14 -> x0, local copies, waits for them, and re-layouts: 8.36 us -> none
    reduce_sum x2 -> x0, other arithmetic: 1.41 us -> none  [the longest x1 1.29 us: tree_tables(): depth = jnp.sum(jnp.where(ordinal <= own_shard, deeper, 0))]
where the time goes in v2:
time: 136 us
  Pallas kernels  135 us (99%)
    pallas_call x1, Pallas kernels, give_back(): pl.pallas_call(functools.partial(return_kernel, shards, heads), out_shape...  50.1 us
    pallas_call x1, Pallas kernels, settle(): pl.pallas_call(settle_kernel, out_shape=[jax.ShapeDtypeStruct(a.shape, a....  48.8 us
    pallas_call x1, Pallas kernels, gather(): pl.pallas_call(functools.partial(gather_kernel, shards, heads, levels), o...  25 us
    pallas_call x1, Pallas kernels, attend(): pl.pallas_call(functools.partial(attend_kernel, levels), out_shape=[jax.S...  10.9 us

profile of v2, /device:TPU:0, one launch (start us, length us, event | category | flops | bytes accessed | tf_op | source)
XLA Modules:
  0.0 135.5 jit_solution(15589382295405843879)
XLA Ops:
  0.6 25.0 %gather.1 = (bf16[256,1024]{1,0:T(8,128)(2,1)}, bf16[256,1024]{1,0:T(8,128)(2,1)}, bf16[9,256,512]{2,1,0:T(8,128)(2,1)}, bf16[9,256,512]{2,1,0:T(8,128)(2,1)}, s...) custom-call(s32[16]{0:T(128)} %gap.1, bf16[128,2048]{1,0:T(8,128)(2,1)} %q.1, bf16[128,1024]{1,0:T(8,128)(2,1)} %k.1, ...), custom_call_target="tpu_custom_call" | custom-call | tf_op jit(solution)/shard_map/gather/pallas_call | solution.py:233
  25.7 10.9 %attend.1 = (bf16[256,1024]{1,0:T(8,128)(2,1)}, bf16[256,1024]{1,0:T(8,128)(2,1)}, bf16[9,256,512]{2,1,0:T(8,128)(2,1)}, bf16[9,256,512]{2,1,0:T(8,128)(2,1)}) custom-call(s32[10]{0:T(128)} %get-tuple-element.19.table, bf16[256,1024]{1,0:T(8,128)(2,1)} %get-tuple-element.20.refs_0_, bf16[256,1024]{1,0:T(8,128)(2,1)} %get-tuple-element.21.refs_1_, ...), custom_call_target="tpu_custom_call" | custom-call | tf_op jit(solution)/shard_map/attend/pallas_call | solution.py:342
  36.6 50.1 %give_back.1 = (bf16[128,2048]{1,0:T(8,128)(2,1)}, bf16[128,2048]{1,0:T(8,128)(2,1)}, bf16[128,1024]{1,0:T(8,128)(2,1)}, bf16[128,1024]{1,0:T(8,128)(2,1)}) custom-call(bf16[256,1024]{1,0:T(8,128)(2,1)} %get-tuple-element.26.out, bf16[256,1024]{1,0:T(8,128)(2,1)} %get-tuple-element.27.grad_q, bf16[9,256,512]{2,1,0:T(8,128)(2,1)} %get-tuple-element.28.part_k, ...), custom_call_target="tpu_custom_call" | custom-call | tf_op jit(solution)/shard_map/give_back/pallas_call | solution.py:540
  86.7 48.8 %settle.1 = (bf16[128,2048]{1,0:T(8,128)(2,1)}, bf16[128,2048]{1,0:T(8,128)(2,1)}, bf16[128,1024]{1,0:T(8,128)(2,1)}, bf16[128,1024]{1,0:T(8,128)(2,1)}) custom-call(bf16[128,2048]{1,0:T(8,128)(2,1)} %get-tuple-element.30.refs_0_, bf16[128,2048]{1,0:T(8,128)(2,1)} %get-tuple-element.31.refs_1_, bf16[128,1024]{1,0:T(8,128)(2,1)} %get-tuple-element.32.refs_2_, ...), custom_call_target="tpu_custom_call" | custom-call | tf_op jit(solution)/shard_map/settle/pallas_call | solution.py:581

commit v3 on v2

--- a/solution.py
+++ b/solution.py
@@ -64,13 +64,15 @@
 
 
 def gather_kernel(
-    shards, heads, levels, gap, q, k, v, g, qh, gh, kb, vb, table, cosine, sine,
-    qi, ki, qr, kr, i_sem, y_send, y_recv, y_local, c_send, c_recv,
+    shards, heads, levels, gap, q, k, v, g, qh, gh, kb_out, vb_out, table, cosine, sine,
+    qi, ki, vi, gi, qr, kr, kb, vb, i_sem, o_sem, y_send, y_recv, y_local, c_send, c_recv,
 ):
-    load_k = pltpu.make_async_copy(k, ki, i_sem.at[0])
-    load_q = pltpu.make_async_copy(q, qi, i_sem.at[1])
-    load_k.start()
-    load_q.start()
+    loads = [
+        pltpu.make_async_copy(src, dst, i_sem.at[i])
+        for i, (src, dst) in enumerate(((k, ki), (v, vi), (q, qi), (g, gi)))
+    ]
+    for i in (1, 0, 2, 3):
+        loads[i].start()
     me, head, core, row = greet(shards, heads)
     rows = q.shape[0]
     tokens = rows * heads
@@ -103,8 +105,17 @@
         local.start()
         exchanged[index] = (copies, local)
 
-    buffers = (kb, vb)
-    sends = []
+    buffers, outputs = (kb, vb), (kb_out, vb_out)
+    sends, stores = [], []
+
+    def store(chunk, slot):
+        kv, step = chunk
+        at = group(step)
+        copy = pltpu.make_async_copy(
+            buffers[kv].at[slot, at, :], outputs[kv].at[slot, at, :], o_sem.at[kv, step, slot]
+        )
+        pl.when(me >= slot)(copy.start)
+        stores.append((me >= slot, copy))
 
     def send(chunk, src, dst, target, *conditions, source=None):
         kv, step = chunk
@@ -125,6 +136,7 @@
             place, place, c_send.at[0], c_recv.at[kv, step, slot], {"ctx": me + 1 - 2 * core}
         )
         pl.when(me >= slot)(copy.wait_recv)
+        store(chunk, slot)
 
     up = me + 4 < shards
 
@@ -133,8 +145,9 @@
         send(chunk, 0, 2, me + 2, row == 0, source=source)
         send(chunk, 0, 1, me + 1, core == 0, source=source)
 
-    first((1, 0), v)
-    exchange(1, v, vb.at[0])
+    loads[1].wait()
+    first((1, 0), vi)
+    exchange(1, vi, vb.at[0])
 
     def count(i, depth):
         return depth + jnp.where(jnp.logical_and(i <= me, gap[i] == 1), 1, 0)
@@ -164,18 +177,23 @@
             at = slice(i * HD, (i + 1) * HD)
             dst[:, at] = turn(src[:, at].astype(jnp.float32), cos, sin).astype(jnp.bfloat16)
 
-    load_k.wait()
+    loads[0].wait()
     rotate(ki, kr)
     exchange(0, kr, kb.at[0])
     first((0, 0), kr)
-    load_q.wait()
+    loads[2].wait()
     rotate(qi, qr)
     for step in range(1, heads):
         for kv in (1, 0):
             exchanged[kv][0][heads - step - 1].wait_recv()
             first((kv, step))
+            store((kv, step), 0)
     exchange(2, qr, qh)
-    exchange(3, g, gh)
+    loads[3].wait()
+    exchange(3, gi, gh)
+    for kv in (1, 0):
+        exchanged[kv][1].wait()
+        store((kv, 0), 0)
 
     def second(chunk):
         received(chunk, 4)
@@ -209,7 +227,8 @@
                 behind(before)
     for index in range(4):
         copies, local = exchanged[index]
-        local.wait()
+        if index > 1:
+            local.wait()
         for copy in copies:
             copy.wait_send()
             if index > 1:
@@ -219,6 +238,8 @@
             received(chunk, slot)
     for condition, copy in sends:
         pl.when(condition)(copy.wait_send)
+    for condition, copy in stores:
+        pl.when(condition)(copy.wait)
 
 
 def gather(shards, heads, levels, gap, q, k, v, g):
@@ -242,13 +263,18 @@
             angle,
         ],
         in_specs=[smem] + [hbm] * 4,
-        out_specs=[hbm] * 4 + [smem, vmem, vmem],
+        out_specs=[vmem, vmem, hbm, hbm, smem, vmem, vmem],
         scratch_shapes=[
             pltpu.VMEM(q.shape, low),
             pltpu.VMEM(k.shape, low),
+            pltpu.VMEM(v.shape, low),
+            pltpu.VMEM(g.shape, low),
             pltpu.VMEM(q.shape, low),
             pltpu.VMEM(k.shape, low),
-            pltpu.SemaphoreType.DMA((2,)),
+            pltpu.VMEM((SLOTS, tokens, narrow), low),
+            pltpu.VMEM((SLOTS, tokens, narrow), low),
+            pltpu.SemaphoreType.DMA((4,)),
+            pltpu.SemaphoreType.DMA((2, heads, SLOTS)),
             pltpu.SemaphoreType.DMA((4, heads - 1)),
             pltpu.SemaphoreType.DMA((4, heads - 1)),
             pltpu.SemaphoreType.DMA((4,)),
@@ -270,6 +296,7 @@
     scaling = HD**-0.5
     f32, low = jnp.float32, jnp.bfloat16
     query = jnp.concatenate([q[:, i * HD : (i + 1) * HD] for i in range(GROUP)], 0)
+    query = query * jnp.asarray(scaling, low)
     grad = jnp.concatenate([g[:, i * HD : (i + 1) * HD] for i in range(GROUP)], 0)
     across = (((1,), (1,)), ((), ()))
     down = (((0,), (0,)), ((), ()))
@@ -278,16 +305,17 @@
     later = jnp.concatenate([(key_at - query_at).astype(f32)] * GROUP, 0) > 0
     scores = []
     for j in range(levels + 1):
-        s = lax.dot_general(query, keys[j][0], across, preferred_element_type=f32) * scaling
+        s = lax.dot_general(query, keys[j][0], across, preferred_element_type=f32)
         if j == 0:
             s = jnp.where(later, -1e30, s)
-        else:
-            if j == levels:
-                s = jnp.where(later, s, -1e30)
-            s = jnp.where(table[levels + 1 + j] > 0, s, -1e30)
+        elif j == levels:
+            s = jnp.where(later, s, -1e30)
         scores.append(s)
-    highest = functools.reduce(jnp.maximum, [jnp.max(s, -1, keepdims=True) for s in scores])
-    raw = [jnp.exp(s - highest) for s in scores]
+    absent = [jnp.where(table[levels + 1 + j] > 0, 0.0, 1e30) for j in range(levels + 1)]
+    highest = functools.reduce(
+        jnp.maximum, [jnp.max(s, -1, keepdims=True) - a for s, a in zip(scores, absent)]
+    )
+    raw = [jnp.exp(s - (highest + a)) for s, a in zip(scores, absent)]
     total = sum(jnp.sum(r, -1, keepdims=True) for r in raw)
     inverse = 1.0 / total
     probs = [r * inverse for r in raw]
@@ -301,9 +329,9 @@
     ]
     delta = sum(jnp.sum(p * d, -1, keepdims=True) for p, d in zip(probs, grad_probs))
     grad_scores = [
-        (p * (d - delta) * scaling).astype(low) for p, d in zip(probs, grad_probs)
+        (p * (d - delta)).astype(low) for p, d in zip(probs, grad_probs)
     ]
-    turned = sum(
+    turned = scaling * sum(
         lax.dot(d, keys[j][0], preferred_element_type=f32) for j, d in enumerate(grad_scores)
     )
     cos, sin = cosine[...], -sine[...]
@@ -362,11 +390,17 @@
 
 def return_kernel(
     shards, heads, out, grad_q, part_k, part_v, cosine, sine, out_o, out_q, out_k, out_v,
-    acc, from_core, from_row, from_up, done, a_sem, y_send, y_recv, y_local,
+    acc, odd, from_core, from_row, from_up, done, a_sem, b_sem, y_send, y_recv, y_local,
     p_send, p_recv, p_local, c_send, c_recv,
 ):
     parts = (part_k, part_v)
-    loads = {}
+    loads, odd_loads = {}, {}
+    for i in (3, 2, 1, 0):
+        for kv in (0, 1):
+            odd_loads[kv, i] = pltpu.make_async_copy(
+                parts[kv].at[2 * i + 1], odd.at[kv, i], b_sem.at[kv, i]
+            )
+            odd_loads[kv, i].start()
     for at in (3, 4, 1, 2, 0):
         for kv in (0, 1):
             loads[kv, at] = pltpu.make_async_copy(
@@ -408,8 +442,10 @@
         for kv, step in chunks:
             at = group(step)
             for i in pair:
+                if step == 0:
+                    odd_loads[kv, i].wait()
                 core_copies[kv, step, i] = remote(
-                    parts[kv].at[2 * i + 1, at, :], from_core.at[kv, i, at, :],
+                    odd.at[kv, i, at, :], from_core.at[kv, i, at, :],
                     c_send.at[kv, step, i], c_recv.at[kv, step, i],
                     {"ctx": me + 1 - 2 * core},
                 )
@@ -540,15 +576,17 @@
     return pl.pallas_call(
         functools.partial(return_kernel, shards, heads),
         out_shape=[wide_out, wide_out, narrow_out, narrow_out],
-        in_specs=[hbm, hbm, hbm, hbm, vmem, vmem],
-        out_specs=[pl.BlockSpec(memory_space=pl.ANY)] * 4,
+        in_specs=[vmem, vmem, hbm, hbm, vmem, vmem],
+        out_specs=[vmem] * 4,
         scratch_shapes=[
             pltpu.VMEM((2, 5, tokens, narrow), low),
+            pltpu.VMEM((2, 4, tokens, narrow), low),
             pltpu.VMEM((2, 4, tokens, narrow), low),
             pltpu.VMEM((2, 2, tokens, narrow), low),
             pltpu.VMEM((2, 2, tokens, narrow), low),
             pltpu.VMEM((2, tokens, narrow), low),
             pltpu.SemaphoreType.DMA((2, 5)),
+            pltpu.SemaphoreType.DMA((2, 4)),
             pltpu.SemaphoreType.DMA((2, peers)),
             pltpu.SemaphoreType.DMA((2, peers)),
             pltpu.SemaphoreType.DMA((2,)),
@@ -565,25 +603,31 @@
     )(out, grad_q, part_k, part_v, cosine, sine)
 
 
-def settle_kernel(*refs):
-    count = len(refs) // 2
-    copies = [
-        pltpu.make_async_copy(refs[i], refs[count + i], refs[-1].at[i]) for i in range(count)
-    ]
-    for copy in copies:
-        copy.start()
-    for copy in copies:
-        copy.wait()
+def settle_kernel(count, *refs):
+    given, made, held = refs[:count], refs[count : 2 * count], refs[2 * count : 3 * count]
+    into, away = refs[3 * count :]
+    loads = [pltpu.make_async_copy(given[i], held[i], into.at[i]) for i in range(count)]
+    stores = [pltpu.make_async_copy(held[i], made[i], away.at[i]) for i in range(count)]
+    for load in loads:
+        load.start()
+    for load, store in zip(loads, stores):
+        load.wait()
+        store.start()
+    for store in stores:
+        store.wait()
 
 
 def settle(*arrays):
-    space = pl.BlockSpec(memory_space=pl.ANY)
+    count = len(arrays)
+    space = pl.BlockSpec(memory_space=pltpu.HBM)
     return pl.pallas_call(
-        settle_kernel,
+        functools.partial(settle_kernel, count),
         out_shape=[jax.ShapeDtypeStruct(a.shape, a.dtype) for a in arrays],
-        in_specs=[space] * len(arrays),
-        out_specs=[pl.BlockSpec(memory_space=pltpu.HBM)] * len(arrays),
-        scratch_shapes=[pltpu.SemaphoreType.DMA((len(arrays),))],
+        in_specs=[space] * count,
+        out_specs=[space] * count,
+        scratch_shapes=[pltpu.VMEM(a.shape, a.dtype) for a in arrays]
+        + [pltpu.SemaphoreType.DMA((count,))] * 2,
+        compiler_params=pltpu.CompilerParams(vmem_limit_bytes=VMEM_LIMIT),
         name="settle",
     )(*arrays)
 

time: 136 us -> 90.1 us (0.66)
  Pallas kernels: 135 us -> 89.3 us
    pallas_call x1, Pallas kernels: 48.8 us -> 2.25 us  [settle(): pl.pallas_call(functools.partial(settle_kernel, count), out_shape=[jax.Sh...]
where the time goes in v3:
time: 90.1 us; the launch traced here: 89.9 us
  Pallas kernels  89.3 us (99%)
    pallas_call x1, Pallas kernels, give_back(): pl.pallas_call(functools.partial(return_kernel, shards, heads), out_shape...  50.5 us
    pallas_call x1, Pallas kernels, gather(): pl.pallas_call(functools.partial(gather_kernel, shards, heads, levels), o...  25.3 us
    pallas_call x1, Pallas kernels, attend(): pl.pallas_call(functools.partial(attend_kernel, levels), out_shape=[jax.S...  11.1 us
    pallas_call x1, Pallas kernels, settle(): pl.pallas_call(functools.partial(settle_kernel, count), out_shape=[jax.Sh...  2.25 us

profile of v3, /device:TPU:0, one launch (start us, length us, event | category | flops | bytes accessed | tf_op | source)
XLA Modules:
  0.0 89.9 jit_solution(4007470239143273212)
XLA Ops:
  0.6 25.3 %gather.1 = (bf16[256,1024]{1,0:T(8,128)(2,1)}, bf16[256,1024]{1,0:T(8,128)(2,1)}, bf16[9,256,512]{2,1,0:T(8,128)(2,1)}, bf16[9,256,512]{2,1,0:T(8,128)(2,1)}, s...) custom-call(s32[16]{0:T(128)} %gap.1, bf16[128,2048]{1,0:T(8,128)(2,1)} %q.1, bf16[128,1024]{1,0:T(8,128)(2,1)} %k.1, ...), custom_call_target="tpu_custom_call" | custom-call | tf_op jit(solution)/shard_map/gather/pallas_call | solution.py:254
  26.0 11.1 %attend.1 = (bf16[256,1024]{1,0:T(8,128)(2,1)}, bf16[256,1024]{1,0:T(8,128)(2,1)}, bf16[9,256,512]{2,1,0:T(8,128)(2,1)}, bf16[9,256,512]{2,1,0:T(8,128)(2,1)}) custom-call(s32[10]{0:T(128)} %get-tuple-element.19.table, bf16[256,1024]{1,0:T(8,128)(2,1)} %get-tuple-element.20.refs_0_, bf16[256,1024]{1,0:T(8,128)(2,1)} %get-tuple-element.21.refs_1_, ...), custom_call_target="tpu_custom_call" | custom-call | tf_op jit(solution)/shard_map/attend/pallas_call | solution.py:370
  37.1 50.5 %give_back.1 = (bf16[128,2048]{1,0:T(8,128)(2,1)}, bf16[128,2048]{1,0:T(8,128)(2,1)}, bf16[128,1024]{1,0:T(8,128)(2,1)}, bf16[128,1024]{1,0:T(8,128)(2,1)}) custom-call(bf16[256,1024]{1,0:T(8,128)(2,1)} %get-tuple-element.26.out, bf16[256,1024]{1,0:T(8,128)(2,1)} %get-tuple-element.27.grad_q, bf16[9,256,512]{2,1,0:T(8,128)(2,1)} %get-tuple-element.28.part_k, ...), custom_call_target="tpu_custom_call" | custom-call | tf_op jit(solution)/shard_map/give_back/pallas_call | solution.py:576
  87.7 2.2 %settle.1 = (bf16[128,2048]{1,0:T(8,128)(2,1)}, bf16[128,2048]{1,0:T(8,128)(2,1)}, bf16[128,1024]{1,0:T(8,128)(2,1)}, bf16[128,1024]{1,0:T(8,128)(2,1)}) custom-call(bf16[128,2048]{1,0:T(8,128)(2,1)} %get-tuple-element.30.refs_0_, bf16[128,2048]{1,0:T(8,128)(2,1)} %get-tuple-element.31.refs_1_, bf16[128,1024]{1,0:T(8,128)(2,1)} %get-tuple-element.32.refs_2_, ...), custom_call_target="tpu_custom_call" | custom-call | tf_op jit(solution)/shard_map/settle/pallas_call | solution.py:623

commit v4 on v3

--- a/solution.py
+++ b/solution.py
@@ -14,6 +14,7 @@
 FORK = 2
 BASE = 10000.0
 SLOTS = 9
+SPLIT = 2
 VMEM_LIMIT = 60 * 2**20
 MESH = pl.DeviceIdType.MESH
 
@@ -80,9 +81,16 @@
     def group(step):
         return pl.ds(pl.multiple_of(lax.rem(head + step, heads) * rows, rows), rows)
 
-    def own_columns(src):
+    def piece(step):
+        size = rows // SPLIT
+        start = lax.rem(head + step // SPLIT, heads) * rows + step % SPLIT * size
+        return pl.ds(pl.multiple_of(start, size), size)
+
+    def own_columns(src, step=None):
         width = src.shape[1] // heads
-        return src.at[:, pl.ds(pl.multiple_of(head * width, width), width)]
+        size = rows // SPLIT
+        at = slice(None) if step is None else slice(step * size, (step + 1) * size)
+        return src.at[at, pl.ds(pl.multiple_of(head * width, width), width)]
 
     mine = group(0)
     exchanged = {}
@@ -110,7 +118,7 @@
 
     def store(chunk, slot):
         kv, step = chunk
-        at = group(step)
+        at = piece(step)
         copy = pltpu.make_async_copy(
             buffers[kv].at[slot, at, :], outputs[kv].at[slot, at, :], o_sem.at[kv, step, slot]
         )
@@ -119,9 +127,9 @@
 
     def send(chunk, src, dst, target, *conditions, source=None):
         kv, step = chunk
-        at = group(step)
+        at = piece(step)
         copy = remote(
-            buffers[kv].at[src, at, :] if source is None else own_columns(source),
+            buffers[kv].at[src, at, :] if source is None else own_columns(source, step),
             buffers[kv].at[dst, at, :],
             c_send.at[len(sends)], c_recv.at[kv, step, dst], {"ctx": target},
         )
@@ -131,7 +139,7 @@
 
     def received(chunk, slot):
         kv, step = chunk
-        place = buffers[kv].at[slot, group(step), :]
+        place = buffers[kv].at[slot, piece(step), :]
         copy = remote(
             place, place, c_send.at[0], c_recv.at[kv, step, slot], {"ctx": me + 1 - 2 * core}
         )
@@ -146,7 +154,8 @@
         send(chunk, 0, 1, me + 1, core == 0, source=source)
 
     loads[1].wait()
-    first((1, 0), vi)
+    for part in range(SPLIT):
+        first((1, part), vi)
     exchange(1, vi, vb.at[0])
 
     def count(i, depth):
@@ -180,20 +189,23 @@
     loads[0].wait()
     rotate(ki, kr)
     exchange(0, kr, kb.at[0])
-    first((0, 0), kr)
+    for part in range(SPLIT):
+        first((0, part), kr)
     loads[2].wait()
     rotate(qi, qr)
     for step in range(1, heads):
         for kv in (1, 0):
             exchanged[kv][0][heads - step - 1].wait_recv()
-            first((kv, step))
-            store((kv, step), 0)
+            for part in range(SPLIT):
+                first((kv, step * SPLIT + part))
+                store((kv, step * SPLIT + part), 0)
     exchange(2, qr, qh)
     loads[3].wait()
     exchange(3, gi, gh)
     for kv in (1, 0):
         exchanged[kv][1].wait()
-        store((kv, 0), 0)
+        for part in range(SPLIT):
+            store((kv, part), 0)
 
     def second(chunk):
         received(chunk, 4)
@@ -218,7 +230,7 @@
         send(chunk, 6, 7, me + 1, core == 0)
         send(chunk, 6, 5, me - 1, core == 1)
 
-    chunks = [(kv, step) for step in range(heads) for kv in (1, 0)]
+    chunks = [(kv, step) for step in range(SPLIT * heads) for kv in (1, 0)]
     for ahead, behind in ((second, across), (third, last)):
         for chunk, before in zip(chunks + [None], [None] + chunks):
             if chunk is not None:
@@ -274,12 +286,12 @@
             pltpu.VMEM((SLOTS, tokens, narrow), low),
             pltpu.VMEM((SLOTS, tokens, narrow), low),
             pltpu.SemaphoreType.DMA((4,)),
-            pltpu.SemaphoreType.DMA((2, heads, SLOTS)),
+            pltpu.SemaphoreType.DMA((2, SPLIT * heads, SLOTS)),
             pltpu.SemaphoreType.DMA((4, heads - 1)),
             pltpu.SemaphoreType.DMA((4, heads - 1)),
             pltpu.SemaphoreType.DMA((4,)),
-            pltpu.SemaphoreType.DMA((28 * heads,)),
-            pltpu.SemaphoreType.DMA((2, heads, SLOTS)),
+            pltpu.SemaphoreType.DMA((28 * SPLIT * heads,)),
+            pltpu.SemaphoreType.DMA((2, SPLIT * heads, SLOTS)),
         ],
         compiler_params=pltpu.CompilerParams(
             collective_id=0, has_side_effects=True, vmem_limit_bytes=VMEM_LIMIT
@@ -415,6 +427,11 @@
     def group(step):
         return pl.ds(pl.multiple_of(lax.rem(head + 1 + step, heads) * rows, rows), rows)
 
+    def piece(step):
+        size = rows // SPLIT
+        start = lax.rem(head + 1 + step // SPLIT, heads) * rows + step % SPLIT * size
+        return pl.ds(pl.multiple_of(start, size), size)
+
     def exchange(src, dst):
         index = len(exchanged)
         width = src.shape[1]
@@ -436,11 +453,11 @@
         local.start()
         exchanged.append((copies, local))
 
-    chunks = [(kv, step) for step in range(heads) for kv in (0, 1)]
+    chunks = [(kv, step) for step in range(SPLIT * heads) for kv in (0, 1)]
     core_copies, row_copies, down_copies = {}, {}, {}
     for pair in ((3, 2), (1, 0)):
         for kv, step in chunks:
-            at = group(step)
+            at = piece(step)
             for i in pair:
                 if step == 0:
                     odd_loads[kv, i].wait()
@@ -453,7 +470,7 @@
 
     def to_row(chunk, i, slot):
         kv, step = chunk
-        at = group(step)
+        at = piece(step)
         row_copies[kv, step, i] = remote(
             acc.at[kv, slot // 2, at, :], from_row.at[kv, i, at, :],
             c_send.at[kv, step, 4 + i], c_recv.at[kv, step, 4 + i],
@@ -465,7 +482,7 @@
 
     def to_down(chunk, i, slot):
         kv, step = chunk
-        at = group(step)
+        at = piece(step)
         down_copies[kv, step, i] = remote(
             acc.at[kv, slot // 2, at, :], from_up.at[kv, i, at, :],
             c_send.at[kv, step, 6 + i], c_recv.at[kv, step, 6 + i], {"ctx": me - 4},
@@ -474,7 +491,7 @@
 
     def add(chunk, slot, pieces, i):
         kv, step = chunk
-        at = group(step)
+        at = piece(step)
         total = acc[kv, slot // 2, at, :].astype(f32) + pieces[kv, i, at, :].astype(f32)
         acc[kv, slot // 2, at, :] = total.astype(low)
 
@@ -520,7 +537,7 @@
 
     def final(chunk):
         kv, step = chunk
-        at = group(step)
+        at = piece(step)
 
         @pl.when(has_up)
         def _():
@@ -535,13 +552,15 @@
         else:
             done[kv, at, :] = acc[kv, 0, at, :]
         width = acc.shape[3]
-        dst = (out_k, out_v)[kv].at[:, pl.ds(pl.multiple_of(head * width, width), width)]
-        if step == heads - 1:
-            copy = pltpu.make_async_copy(done.at[kv, at, :], dst, p_local.at[kv])
+        size = rows // SPLIT
+        part = slice(step % SPLIT * size, (step % SPLIT + 1) * size)
+        dst = (out_k, out_v)[kv].at[part, pl.ds(pl.multiple_of(head * width, width), width)]
+        if step // SPLIT == heads - 1:
+            copy = pltpu.make_async_copy(done.at[kv, at, :], dst, p_local.at[kv, step % SPLIT])
         else:
             copy = remote(
                 done.at[kv, at, :], dst, p_send.at[kv, step], p_recv.at[kv, step],
-                {"head": lax.rem(head + 1 + step, heads)},
+                {"head": lax.rem(head + 1 + step // SPLIT, heads)},
             )
         copy.start()
         finals.append(copy)
@@ -590,11 +609,11 @@
             pltpu.SemaphoreType.DMA((2, peers)),
             pltpu.SemaphoreType.DMA((2, peers)),
             pltpu.SemaphoreType.DMA((2,)),
-            pltpu.SemaphoreType.DMA((2, peers)),
-            pltpu.SemaphoreType.DMA((2, peers)),
-            pltpu.SemaphoreType.DMA((2,)),
-            pltpu.SemaphoreType.DMA((2, heads, 8)),
-            pltpu.SemaphoreType.DMA((2, heads, 8)),
+            pltpu.SemaphoreType.DMA((2, SPLIT * peers)),
+            pltpu.SemaphoreType.DMA((2, SPLIT * peers)),
+            pltpu.SemaphoreType.DMA((2, SPLIT)),
+            pltpu.SemaphoreType.DMA((2, SPLIT * heads, 8)),
+            pltpu.SemaphoreType.DMA((2, SPLIT * heads, 8)),
         ],
         compiler_params=pltpu.CompilerParams(
             collective_id=1, has_side_effects=True, vmem_limit_bytes=VMEM_LIMIT

time: 90.1 us -> 94.7 us (1.051)
  Pallas kernels: 89.3 us -> 93.8 us
    pallas_call x1, Pallas kernels: 50.5 us -> 53.8 us  [give_back(): pl.pallas_call(functools.partial(return_kernel, shards, heads), out_shape...]
    pallas_call x1, Pallas kernels: 25.3 us -> 26.6 us  [gather(): pl.pallas_call(functools.partial(gather_kernel, shards, heads, levels), o...]
where the time goes in v4:
time: 94.7 us; the launch traced here: 94.5 us
  Pallas kernels  93.8 us (99%)
    pallas_call x1, Pallas kernels, give_back(): pl.pallas_call(functools.partial(return_kernel, shards, heads), out_shape...  53.8 us
    pallas_call x1, Pallas kernels, gather(): pl.pallas_call(functools.partial(gather_kernel, shards, heads, levels), o...  26.6 us
    pallas_call x1, Pallas kernels, attend(): pl.pallas_call(functools.partial(attend_kernel, levels), out_shape=[jax.S...  11.1 us
    pallas_call x1, Pallas kernels, settle(): pl.pallas_call(functools.partial(settle_kernel, count), out_shape=[jax.Sh...  2.25 us

profile of v4, /device:TPU:0, one launch (start us, length us, event | category | flops | bytes accessed | tf_op | source)
XLA Modules:
  0.0 94.5 jit_solution(17890804285430641451)
XLA Ops:
  0.6 26.6 %gather.1 = (bf16[256,1024]{1,0:T(8,128)(2,1)}, bf16[256,1024]{1,0:T(8,128)(2,1)}, bf16[9,256,512]{2,1,0:T(8,128)(2,1)}, bf16[9,256,512]{2,1,0:T(8,128)(2,1)}, s...) custom-call(s32[16]{0:T(128)} %gap.1, bf16[128,2048]{1,0:T(8,128)(2,1)} %q.1, bf16[128,1024]{1,0:T(8,128)(2,1)} %k.1, ...), custom_call_target="tpu_custom_call" | custom-call | tf_op jit(solution)/shard_map/gather/pallas_call | solution.py:266
  27.2 11.1 %attend.1 = (bf16[256,1024]{1,0:T(8,128)(2,1)}, bf16[256,1024]{1,0:T(8,128)(2,1)}, bf16[9,256,512]{2,1,0:T(8,128)(2,1)}, bf16[9,256,512]{2,1,0:T(8,128)(2,1)}) custom-call(s32[10]{0:T(128)} %get-tuple-element.19.table, bf16[256,1024]{1,0:T(8,128)(2,1)} %get-tuple-element.20.refs_0_, bf16[256,1024]{1,0:T(8,128)(2,1)} %get-tuple-element.21.refs_1_, ...), custom_call_target="tpu_custom_call" | custom-call | tf_op jit(solution)/shard_map/attend/pallas_call | solution.py:382
  38.4 53.8 %give_back.1 = (bf16[128,2048]{1,0:T(8,128)(2,1)}, bf16[128,2048]{1,0:T(8,128)(2,1)}, bf16[128,1024]{1,0:T(8,128)(2,1)}, bf16[128,1024]{1,0:T(8,128)(2,1)}) custom-call(bf16[256,1024]{1,0:T(8,128)(2,1)} %get-tuple-element.26.out, bf16[256,1024]{1,0:T(8,128)(2,1)} %get-tuple-element.27.grad_q, bf16[9,256,512]{2,1,0:T(8,128)(2,1)} %get-tuple-element.28.part_k, ...), custom_call_target="tpu_custom_call" | custom-call | tf_op jit(solution)/shard_map/give_back/pallas_call | solution.py:595
  92.3 2.2 %settle.1 = (bf16[128,2048]{1,0:T(8,128)(2,1)}, bf16[128,2048]{1,0:T(8,128)(2,1)}, bf16[128,1024]{1,0:T(8,128)(2,1)}, bf16[128,1024]{1,0:T(8,128)(2,1)}) custom-call(bf16[128,2048]{1,0:T(8,128)(2,1)} %get-tuple-element.30.refs_0_, bf16[128,2048]{1,0:T(8,128)(2,1)} %get-tuple-element.31.refs_1_, bf16[128,1024]{1,0:T(8,128)(2,1)} %get-tuple-element.32.refs_2_, ...), custom_call_target="tpu_custom_call" | custom-call | tf_op jit(solution)/shard_map/settle/pallas_call | solution.py:642
